TPU v7x, 128 devices: a whole 4x4x4 slice. The times are simulated.
128 devices in a mesh: ctx: 16 (over z_lo, x, core), ch: 8 (over z_hi, y).
Axes of the slice: x: 4, y: 4, z: 4 (z_hi: 2, z_lo: 2; z = z_hi * 2 + z_lo), core: 2. Of those that a mesh axis runs over, the one named last changes fastest.
Arguments:
- signal: bfloat16 [128, 262144], P('ch', 'ctx'), may hold values from -6 to 6
- gate: bfloat16 [128, 262144], P('ch', 'ctx'), may hold values from -6 to 6
- cotangent: bfloat16 [128, 262144], P('ch', 'ctx'), may hold values from -6 to 6
- skip_gain: float32 [128], P('ch'), may hold values from 0.5 to 1.5
- filter_taps: float32 [16, 262144], P(None, 'ctx'), may hold values from -0.01171875 to 0.01171875
Outputs:
- output: bfloat16 [128, 262144], P('ch', 'ctx')
- grad_gate: bfloat16 [128, 262144], P('ch', 'ctx')
- grad_signal: bfloat16 [128, 262144], P('ch', 'ctx')
- grad_taps: float32 [16, 262144], P('ch', 'ctx')
All inputs are finite; a program needn't handle non-finite values.
Results may differ from a plain program's by a relative error of at most 0.017.
Values may be sent and summed in bfloat16 or wider, within the bound.
A program may use at most 128 MiB of HBM per device.

v0:
```python
import math

import jax
import jax.numpy as jnp
from jax import lax
from jax.sharding import PartitionSpec as P

N1 = 1024
N2 = 512
SEQ = 262144


def cosine_sine(row_values, col_values, period):
    angle_value = (row_values[:, None] * col_values[None, :] % period).astype(jnp.float32) * (
        2.0 * math.pi / period
    )
    return (jnp.cos(angle_value), jnp.sin(angle_value))


def complex_product(former, latter, half_len):
    former_real = former[..., :half_len]
    former_imag = former[..., half_len:]
    latter_real = latter[..., :half_len]
    latter_imag = latter[..., half_len:]
    real_part = former_real * latter_real - former_imag * latter_imag
    imag_part = former_real * latter_imag + former_imag * latter_real
    return jnp.concatenate([real_part, imag_part], axis=-1)


def conjugate_product(former, latter, half_len):
    former_real = former[..., :half_len]
    former_imag = former[..., half_len:]
    latter_real = latter[..., :half_len]
    latter_imag = latter[..., half_len:]
    real_part = former_real * latter_real + former_imag * latter_imag
    imag_part = former_imag * latter_real - former_real * latter_imag
    return jnp.concatenate([real_part, imag_part], axis=-1)


def body(signal, gate, cotangent, skip_gain, filter_taps):
    shards = lax.axis_size("ctx")
    ctx_rank = lax.axis_index("ctx")
    channels = signal.shape[0]
    groups = filter_taps.shape[0]
    half_rows = N1 // 2
    rows_dev = half_rows // shards
    cols_dev = N2 // shards
    freq_dev = N1 // shards
    points = N1 * N2
    n1_index = jnp.arange(half_rows, dtype=jnp.int32)
    k1_index = jnp.arange(N1, dtype=jnp.int32)
    n2_index = jnp.arange(N2, dtype=jnp.int32)
    cos_row, sin_row = cosine_sine(k1_index, n1_index, N1)
    exact_matrix = jnp.concatenate([cos_row, -sin_row], axis=0)
    section_matrix = exact_matrix.astype(jnp.bfloat16)
    cos_b, sin_b = cosine_sine(n2_index, n2_index, N2)
    two_real = jnp.concatenate([cos_b, -sin_b], axis=1).astype(jnp.bfloat16)
    two_imag = jnp.concatenate([sin_b, cos_b], axis=1).astype(jnp.bfloat16)
    back_matrix = jnp.concatenate(
        [jnp.concatenate([cos_b, sin_b], axis=1), jnp.concatenate([-sin_b, cos_b], axis=1)], axis=0
    ).astype(jnp.bfloat16)
    cos_c, sin_c = cosine_sine(n1_index, k1_index, N1)
    back_real = (cos_c / points).astype(jnp.bfloat16)
    back_imag = (-sin_c / points).astype(jnp.bfloat16)
    k1_own = ctx_rank * freq_dev + jnp.arange(freq_dev, dtype=jnp.int32)
    row_cos, row_sin = cosine_sine(k1_own, n2_index, points)
    row_cos = row_cos[:, None, :]
    row_sin = row_sin[:, None, :]

    def twiddle_columns(chan_count):
        col_n2 = (
            ctx_rank * cols_dev + jnp.arange(cols_dev * chan_count, dtype=jnp.int32) // chan_count
        )
        return cosine_sine(k1_index, col_n2, points)

    def rows_to_grid(values):
        chan_count = values.shape[0]
        moved = jnp.transpose(values.reshape(chan_count, rows_dev, N2), (1, 2, 0))
        return moved.reshape(rows_dev, shards, cols_dev * chan_count)

    def grid_to_rows(values, chan_count):
        moved = jnp.transpose(values.reshape(rows_dev, N2, chan_count), (2, 0, 1))
        return moved.reshape(chan_count, rows_dev * N2)

    def to_blocks(values):
        return values.reshape(shards, rows_dev, values.shape[1])

    def first_section(columns, matrix, chan_count, exact_sums):
        columns = columns.reshape(half_rows, cols_dev * chan_count)
        if exact_sums:
            summed = jnp.dot(matrix, columns, precision=lax.Precision.HIGHEST)
        else:
            summed = jnp.dot(matrix, columns, preferred_element_type=jnp.float32)
        twist_cos, twist_sin = twiddle_columns(chan_count)
        real_part = summed[:N1] * twist_cos + summed[N1:] * twist_sin
        imag_part = summed[N1:] * twist_cos - summed[:N1] * twist_sin
        real_part = real_part.astype(jnp.bfloat16).reshape(shards, freq_dev, cols_dev * chan_count)
        imag_part = imag_part.astype(jnp.bfloat16).reshape(shards, freq_dev, cols_dev * chan_count)
        return (real_part, imag_part)

    def second_section(real_part, imag_part):
        item_count = real_part.shape[1]
        chan_count = real_part.shape[2] // N2

        def arrange(part):
            moved = jnp.transpose(part.reshape(item_count, N2, chan_count), (0, 2, 1))
            return moved.reshape(item_count * chan_count, N2)

        spectrum = jnp.dot(
            arrange(real_part), two_real, preferred_element_type=jnp.float32
        ) + jnp.dot(arrange(imag_part), two_imag, preferred_element_type=jnp.float32)
        return spectrum.reshape(item_count, chan_count, 2 * N2)

    def finish_two(pieces):
        return second_section(pieces[0], pieces[1])

    def back_section(product):
        chan_count = product.shape[1]
        rounded = product.astype(jnp.bfloat16).reshape(freq_dev * chan_count, 2 * N2)
        summed = jnp.dot(rounded, back_matrix, preferred_element_type=jnp.float32)
        summed = summed.reshape(freq_dev, chan_count, 2 * N2)
        sum_real = summed[..., :N2]
        sum_imag = summed[..., N2:]
        real_part = (sum_real * row_cos - sum_imag * row_sin).astype(jnp.bfloat16)
        imag_part = (sum_real * row_sin + sum_imag * row_cos).astype(jnp.bfloat16)

        def arrange(part):
            return jnp.transpose(part, (0, 2, 1)).reshape(freq_dev, shards, cols_dev * chan_count)

        return (arrange(real_part), arrange(imag_part))

    def last_section(real_part, imag_part):
        item_count = real_part.shape[2]
        return jnp.dot(
            back_real, real_part.reshape(N1, item_count), preferred_element_type=jnp.float32
        ) + jnp.dot(
            back_imag, imag_part.reshape(N1, item_count), preferred_element_type=jnp.float32
        )

    def finish_one(pieces):
        return last_section(pieces[0], pieces[1])

    tap_cols = lax.all_to_all(
        rows_to_grid(filter_taps), "ctx", split_axis=1, concat_axis=0, tiled=True
    )
    taps_real, taps_imag = first_section(tap_cols, exact_matrix, groups, True)
    filter_spec = finish_two(
        (
            lax.all_to_all(taps_real, "ctx", split_axis=0, concat_axis=2, tiled=True),
            lax.all_to_all(taps_imag, "ctx", split_axis=0, concat_axis=2, tiled=True),
        )
    )
    upstream = gate.astype(jnp.float32) * cotangent.astype(jnp.float32)
    up_half = upstream.astype(jnp.bfloat16)

    def spectrum_of(values):
        columns = lax.all_to_all(
            rows_to_grid(values), "ctx", split_axis=1, concat_axis=0, tiled=True
        )
        real_part, imag_part = first_section(columns, section_matrix, channels, False)
        return finish_two(
            (
                lax.all_to_all(real_part, "ctx", split_axis=0, concat_axis=2, tiled=True),
                lax.all_to_all(imag_part, "ctx", split_axis=0, concat_axis=2, tiled=True),
            )
        )

    def columns_of(product):
        real_part, imag_part = back_section(product)
        return finish_one(
            (
                lax.all_to_all(real_part, "ctx", split_axis=1, concat_axis=0, tiled=True),
                lax.all_to_all(imag_part, "ctx", split_axis=1, concat_axis=0, tiled=True),
            )
        )

    def rows_of(columns):
        blocks = lax.all_to_all(
            to_blocks(columns.astype(jnp.bfloat16)), "ctx", split_axis=0, concat_axis=2, tiled=True
        )
        return grid_to_rows(blocks, channels)

    spec_signal = spectrum_of(signal)
    conv_rows = rows_of(columns_of(complex_product(spec_signal, filter_spec, N2)))
    spec_up = spectrum_of(up_half)
    corr_rows = rows_of(columns_of(conjugate_product(spec_up, filter_spec, N2)))
    taps_cols = columns_of(conjugate_product(spec_up, spec_signal, N2))
    mixed_sum = conv_rows.astype(jnp.float32) + skip_gain[:, None] * signal.astype(jnp.float32)
    output = (gate.astype(jnp.float32) * mixed_sum).astype(jnp.bfloat16)
    grad_gate = (cotangent.astype(jnp.float32) * mixed_sum).astype(jnp.bfloat16)
    grad_signal = (corr_rows.astype(jnp.float32) + skip_gain[:, None] * upstream).astype(
        jnp.bfloat16
    )
    taps_grid = lax.all_to_all(
        to_blocks(taps_cols).astype(jnp.bfloat16), "ctx", split_axis=0, concat_axis=2, tiled=True
    ).astype(jnp.float32)
    taps_rows = grid_to_rows(taps_grid, channels)
    group_total = lax.psum_scatter(
        taps_rows.astype(jnp.bfloat16), "ch", scatter_dimension=0, tiled=True
    ).astype(jnp.float32)
    grad_taps = group_total / math.sqrt(SEQ)
    return (output, grad_gate, grad_signal, grad_taps)


def solution(mesh):
    return jax.shard_map(
        body,
        mesh=mesh,
        in_specs=(P("ch", "ctx"), P("ch", "ctx"), P("ch", "ctx"), P("ch"), P(None, "ctx")),
        out_specs=(P("ch", "ctx"), P("ch", "ctx"), P("ch", "ctx"), P("ch", "ctx")),
        check_vma=False,
    )
```

profile of v0, /device:TPU:0, one launch (start us, length us, event | category | flops | bytes accessed | tf_op | source)
XLA Modules:
  0.0 558.1 jit_solution(15520623289482063676)
XLA Ops:
  12.1 5.8 %all-to-all-start.9 = ((bf16[32,16,512]{2,0,1:T(8,128)(2,1)}), bf16[32,16,512]{2,0,1:T(8,128)(2,1)S(1)}, u32[]{:S(2)}, u32[]{:S(2)}) async-start(bf16[32,16,512]{2,0,1:T(8,128)(2,1)} %copy.97), calls=%async_computation.9 | async-start | bytes 1048576 | tf_op jit(solution)/shard_map/all_to_all | solution.py:157
  22.7 6.2 %all-to-all-done.9 = bf16[32,16,512]{2,0,1:T(8,128)(2,1)S(1)} async-done(((bf16[32,16,512]{2,0,1:T(8,128)(2,1)}), bf16[32,16,512]{2,0,1:T(8,128)(2,1)S(1)}, u32[]{:S(2)}, u32[]{:S(2)}) %all-to-all-start.9) | async-done | bytes 524320 | tf_op jit(solution)/shard_map/all_to_all | solution.py:157
  34.3 3.7 copy.84
  38.0 3.6 copy.85
  43.3 4.2 all-to-all-start.3
  47.5 8.2 %sine_negate_fusion = (f32[1024,512]{1,0:T(8,128)S(1)}, f32[1024,512]{1,0:T(8,128)S(1)}) fusion(), kind=kLoop, calls=%fused_computation.58 | loop fusion | flops 7864320 | bytes 4194304 | tf_op jit(solution)/shard_map/neg | solution.py:54
  63.7 8.9 %fusion = f32[2048,512]{1,0:T(8,128)S(1)} fusion(f32[512,512]{1,0:T(8,128)S(1)} %bitcast.221, f32[1024,512]{1,0:T(8,128)S(1)} %get-tuple-element.37, f32[1024,512]{1,0:T(8,128)} %copy-done.2), kind=kOutput, calls=%fused_computation.1 | convolution fusion | flops 6443499520 | bytes 9437184 | tf_op jit(solution)/shard_map/dot_general | solution.py:91
  72.6 11.3 %subtract_convert_fusion.4 = (bf16[1024,512]{1,0:T(8,128)(2,1)S(1)}, bf16[1024,512]{1,0:T(8,128)(2,1)S(1)}, bf16[1024,512]{1,0:T(8,128)(2,1)}, bf16[1024,512]{1,...) fusion(f32[2048,512]{1,0:T(8,128)S(1)} %copy-done.3, s32[512]{0:T(512)S(1)} %fusion.73, ...), kind=kLoop, calls=%fused_computation.45 | loop fusion | flops 19922944 | bytes 18876416 | tf_op jit(solution)/shard_map/convert_element_type | solution.py:98
  84.0 20.6 %all_to_all.258 = bf16[16,64,512]{2,1,0:T(8,128)(2,1)} all-to-all(bf16[16,64,512]{2,1,0:T(8,128)(2,1)S(1)} %bitcast.225), channel_id=1, replica_groups=mesh['ctx'=16,'ch'=8] {'ctx'}, dimensions={0} | all-to-all | bytes 2097152 | tf_op jit(solution)/shard_map/all_to_all | solution.py:163
  104.6 19.8 %all_to_all.259 = bf16[16,64,512]{2,1,0:T(8,128)(2,1)} all-to-all(bf16[16,64,512]{2,1,0:T(8,128)(2,1)S(1)} %bitcast.224), channel_id=1, replica_groups=mesh['ctx'=16,'ch'=8] {'ctx'}, dimensions={0} | all-to-all | bytes 2097152 | tf_op jit(solution)/shard_map/all_to_all | solution.py:164
  124.3 19.8 %all_to_all.260 = bf16[16,64,512]{2,1,0:T(8,128)(2,1)} all-to-all(bf16[16,64,512]{2,1,0:T(8,128)(2,1)S(1)} %bitcast.223), channel_id=1, replica_groups=mesh['ctx'=16,'ch'=8] {'ctx'}, dimensions={0} | all-to-all | bytes 2097152 | tf_op jit(solution)/shard_map/all_to_all | solution.py:163
  144.1 19.8 %all_to_all.261 = bf16[16,64,512]{2,1,0:T(8,128)(2,1)} all-to-all(bf16[16,64,512]{2,1,0:T(8,128)(2,1)S(1)} %bitcast.222), channel_id=1, replica_groups=mesh['ctx'=16,'ch'=8] {'ctx'}, dimensions={0} | all-to-all | bytes 2097152 | tf_op jit(solution)/shard_map/all_to_all | solution.py:164
  163.9 4.8 all-to-all-start.4
  168.7 4.0 fusion.57
  172.6 5.2 negate_convert_fusion
  180.5 3.6 copy.99
  186.2 3.6 copy.101
  200.9 6.0 %all-to-all-start.5 = ((bf16[16,64,512]{2,1,0:T(8,128)(2,1)}), bf16[16,64,512]{2,1,0:T(8,128)(2,1)}, u32[]{:S(2)}, u32[]{:S(2)}) async-start(bf16[16,64,512]{2,1,0:T(8,128)(2,1)} %bitcast.216), calls=%async_computation.5 | async-start | bytes 2097152 | tf_op jit(solution)/shard_map/all_to_all | solution.py:150
  212.5 4.7 fusion.58
  229.4 3.9 convolution_add_fusion
  247.6 4.9 fusion.45
  252.5 4.3 copy.90
  258.4 5.9 %all-to-all-start.6 = ((bf16[64,16,512]{2,0,1:T(8,128)(2,1)}), bf16[64,16,512]{2,0,1:T(8,128)(2,1)}, u32[]{:S(2)}, u32[]{:S(2)}) async-start(bf16[64,16,512]{2,0,1:T(8,128)(2,1)} %copy.91), calls=%async_computation.6 | async-start | bytes 2097152 | tf_op jit(solution)/shard_map/all_to_all | solution.py:172
  264.3 4.3 copy.92
  270.2 10.6 %all-to-all-done.6 = bf16[64,16,512]{2,0,1:T(8,128)(2,1)} async-done(((bf16[64,16,512]{2,0,1:T(8,128)(2,1)}), bf16[64,16,512]{2,0,1:T(8,128)(2,1)}, u32[]{:S(2)}, u32[]{:S(2)}) %all-to-all-start.6) | async-done | bytes 1048608 | tf_op jit(solution)/shard_map/all_to_all | solution.py:172
  280.8 4.3 all-to-all-start.7
  285.2 4.3 copy.102
  291.1 10.6 %all-to-all-done.7 = bf16[64,16,512]{2,0,1:T(8,128)(2,1)} async-done(((bf16[64,16,512]{2,0,1:T(8,128)(2,1)}), bf16[64,16,512]{2,0,1:T(8,128)(2,1)}, u32[]{:S(2)}, u32[]{:S(2)}) %all-to-all-start.7) | async-done | bytes 1048608 | tf_op jit(solution)/shard_map/all_to_all | solution.py:173
  301.6 4.6 all-to-all-start.12
  306.2 4.3 copy.104
  312.1 10.6 %all-to-all-done.12 = bf16[64,16,512]{2,0,1:T(8,128)(2,1)} async-done(((bf16[64,16,512]{2,0,1:T(8,128)(2,1)}), bf16[64,16,512]{2,0,1:T(8,128)(2,1)}, u32[]{:S(2)}, u32[]{:S(2)}) %all-to-all-start.12) | async-done | bytes 1048608 | tf_op jit(solution)/shard_map/all_to_all | solution.py:172
  322.7 4.3 all-to-all-start.13
  327.1 4.3 copy.108
  333.0 10.6 %all-to-all-done.13 = bf16[64,16,512]{2,0,1:T(8,128)(2,1)} async-done(((bf16[64,16,512]{2,0,1:T(8,128)(2,1)}), bf16[64,16,512]{2,0,1:T(8,128)(2,1)}, u32[]{:S(2)}, u32[]{:S(2)}) %all-to-all-start.13) | async-done | bytes 1048608 | tf_op jit(solution)/shard_map/all_to_all | solution.py:173
  343.6 4.3 all-to-all-start.15
  352.2 12.2 %all-to-all-done.15 = bf16[64,16,512]{2,0,1:T(8,128)(2,1)} async-done(((bf16[64,16,512]{2,0,1:T(8,128)(2,1)}), bf16[64,16,512]{2,0,1:T(8,128)(2,1)}, u32[]{:S(2)}, u32[]{:S(2)}) %all-to-all-start.15) | async-done | bytes 1048608 | tf_op jit(solution)/shard_map/all_to_all | solution.py:172
  364.4 4.1 all-to-all-start.16
  369.8 9.0 %fusion.53 = f32[512,512]{1,0:T(8,128)S(1)} fusion(bf16[1024,512]{1,0:T(8,128)(2,1)} %bitcast.41), kind=kOutput, calls=%fused_computation.105 | convolution fusion | flops 545259520 | bytes 2097152 | tf_op jit(solution)/shard_map/dot_general | solution.py:134
  378.8 10.1 %fusion.32 = bf16[512,512]{1,0:T(8,128)(2,1)} fusion(f32[512,512]{1,0:T(8,128)S(1)} %fusion.53, bf16[1024,512]{1,0:T(8,128)(2,1)} %bitcast.46), kind=kOutput, calls=%fused_computation.76 | convolution fusion | flops 546308096 | bytes 2621440 | tf_op jit(solution)/shard_map/dot_general | solution.py:136
  388.9 5.8 %all-to-all-start.8 = ((bf16[16,32,512]{2,1,0:T(8,128)(2,1)}), bf16[16,32,512]{2,1,0:T(8,128)(2,1)S(1)}, u32[]{:S(2)}, u32[]{:S(2)}) async-start(bf16[16,32,512]{2,1,0:T(8,128)(2,1)} %bitcast.47), calls=%async_computation.8 | async-start | bytes 1048576 | tf_op jit(solution)/shard_map/all_to_all | solution.py:178
  394.7 9.0 %fusion.52 = f32[512,512]{1,0:T(8,128)S(1)} fusion(bf16[1024,512]{1,0:T(8,128)(2,1)} %bitcast.74), kind=kOutput, calls=%fused_computation.104 | convolution fusion | flops 545259520 | bytes 2097152 | tf_op jit(solution)/shard_map/dot_general | solution.py:134
  403.7 10.2 %fusion.33 = bf16[512,512]{1,0:T(8,128)(2,1)} fusion(f32[512,512]{1,0:T(8,128)S(1)} %fusion.52, bf16[1024,512]{1,0:T(8,128)(2,1)} %bitcast.79), kind=kOutput, calls=%fused_computation.77 | convolution fusion | flops 546308096 | bytes 2621440 | tf_op jit(solution)/shard_map/dot_general | solution.py:136
  413.9 5.7 %all-to-all-start.14 = ((bf16[16,32,512]{2,1,0:T(8,128)(2,1)}), bf16[16,32,512]{2,1,0:T(8,128)(2,1)S(1)}, u32[]{:S(2)}, u32[]{:S(2)}) async-start(bf16[16,32,512]{2,1,0:T(8,128)(2,1)} %bitcast.80), calls=%async_computation.14 | async-start | bytes 1048576 | tf_op jit(solution)/shard_map/all_to_all | solution.py:178
  419.6 9.0 %fusion.51 = f32[512,512]{1,0:T(8,128)S(1)} fusion(bf16[1024,512]{1,0:T(8,128)(2,1)} %bitcast.89), kind=kOutput, calls=%fused_computation.103 | convolution fusion | flops 545259520 | bytes 2097152 | tf_op jit(solution)/shard_map/dot_general | solution.py:134
  428.6 9.0 %fusion.34 = bf16[512,512]{1,0:T(8,128)(2,1)} fusion(f32[512,512]{1,0:T(8,128)S(1)} %fusion.51, bf16[1024,512]{1,0:T(8,128)(2,1)S(1)} %bitcast.237), kind=kOutput, calls=%fused_computation.78 | convolution fusion | flops 546308096 | bytes 2621440 | tf_op jit(solution)/shard_map/dot_general | solution.py:136
  437.6 5.8 %all-to-all-start.17 = ((bf16[16,32,512]{2,1,0:T(8,128)(2,1)}), bf16[16,32,512]{2,1,0:T(8,128)(2,1)}, u32[]{:S(2)}, u32[]{:S(2)}) async-start(bf16[16,32,512]{2,1,0:T(8,128)(2,1)} %bitcast.95), calls=%async_computation.17 | async-start | bytes 1048576 | tf_op jit(solution)/shard_map/all_to_all | solution.py:194
  452.6 3.9 copy.118
  464.6 84.6 %all-reduce.3.cloned.1.call-done = bf16[16,16384]{1,0:T(8,128)(2,1)} async-done(((bf16[16,16384]{1,0:T(8,128)(2,1)}), bf16[16,16384]{1,0:T(8,128)(2,1)}) %all-reduce.3.cloned.1.call-update) | async-done | bytes 524304
  (94 shorter events, 104.4 us)
Async XLA Ops:
  12.1 16.7 %all-to-all-start.9 = ((bf16[32,16,512]{2,0,1:T(8,128)(2,1)}), bf16[32,16,512]{2,0,1:T(8,128)(2,1)S(1)}, u32[]{:S(2)}, u32[]{:S(2)}) async-start(bf16[32,16,512]{2,0,1:T(8,128)(2,1)} %copy.97), calls=%async_computation.9 | async-start | bytes 1048576 | tf_op jit(solution)/shard_map/all_to_all | solution.py:157
  28.9 9.1 %copy-start.11 = (bf16[32,16,512]{2,0,1:T(8,128)(2,1)}, bf16[32,16,512]{2,0,1:T(8,128)(2,1)S(1)}, u32[]{:S(2)}) copy-start(bf16[32,16,512]{2,0,1:T(8,128)(2,1)S(1)} %all-to-all-done.9) | copy-start | bytes 1572868
  28.9 14.4 %all-to-all-start = ((bf16[32,16,512]{2,0,1:T(8,128)(2,1)}), bf16[32,16,512]{2,0,1:T(8,128)(2,1)S(1)}, u32[]{:S(2)}, u32[]{:S(2)}) async-start(bf16[32,16,512]{2,0,1:T(8,128)(2,1)} %copy.79), calls=%async_computation | async-start | bytes 1048576 | tf_op jit(solution)/shard_map/all_to_all | solution.py:157
  43.3 4.2 copy-start.13
  43.3 20.5 %all-to-all-start.3 = ((f32[32,16,512]{2,0,1:T(8,128)}), f32[32,16,512]{2,0,1:T(8,128)S(1)}, u32[]{:S(2)}, u32[]{:S(2)}) async-start(f32[32,16,512]{2,0,1:T(8,128)} %copy.85), calls=%async_computation.3 | async-start | bytes 2097152 | tf_op jit(solution)/shard_map/all_to_all | solution.py:143
  47.5 8.3 %copy-start.12 = (bf16[32,16,512]{2,0,1:T(8,128)(2,1)S(1)}, bf16[32,16,512]{2,0,1:T(8,128)(2,1)}, u32[]{:S(2)}) copy-start(bf16[32,16,512]{2,0,1:T(8,128)(2,1)} %copy-done.11) | copy-start | bytes 1572868
  55.7 3.3 copy-start.2
  55.8 3.3 copy-start.14
  63.7 8.9 %copy-start.3 = (f32[2048,512]{1,0:T(8,128)S(1)}, f32[2048,512]{1,0:T(8,128)}, u32[]{:S(2)}) copy-start(f32[2048,512]{1,0:T(8,128)} %fusion.61) | copy-start | bytes 12582916
  63.7 8.9 %copy-start.4 = (f32[2048,512]{1,0:T(8,128)S(1)}, f32[2048,512]{1,0:T(8,128)}, u32[]{:S(2)}) copy-start(f32[2048,512]{1,0:T(8,128)} %fusion.63) | copy-start | bytes 12582916
  163.9 37.1 %all-to-all-start.4 = ((bf16[16,64,512]{2,1,0:T(8,128)(2,1)}), bf16[16,64,512]{2,1,0:T(8,128)(2,1)}, u32[]{:S(2)}, u32[]{:S(2)}) async-start(bf16[16,64,512]{2,1,0:T(8,128)(2,1)} %bitcast.23), calls=%async_computation.4 | async-start | bytes 2097152 | tf_op jit(solution)/shard_map/all_to_all | solution.py:149
  200.9 22.9 %all-to-all-start.5 = ((bf16[16,64,512]{2,1,0:T(8,128)(2,1)}), bf16[16,64,512]{2,1,0:T(8,128)(2,1)}, u32[]{:S(2)}, u32[]{:S(2)}) async-start(bf16[16,64,512]{2,1,0:T(8,128)(2,1)} %bitcast.216), calls=%async_computation.5 | async-start | bytes 2097152 | tf_op jit(solution)/shard_map/all_to_all | solution.py:150
  212.5 4.7 copy-start.5
  212.5 4.7 copy-start.9
  217.2 3.3 copy-start.10
  229.4 3.9 copy-start
  229.4 4.0 copy-start.7
  233.5 2.2 copy-start.1
  233.5 2.5 copy-start.8
  238.4 2.2 copy-start.6
  258.4 22.4 %all-to-all-start.6 = ((bf16[64,16,512]{2,0,1:T(8,128)(2,1)}), bf16[64,16,512]{2,0,1:T(8,128)(2,1)}, u32[]{:S(2)}, u32[]{:S(2)}) async-start(bf16[64,16,512]{2,0,1:T(8,128)(2,1)} %copy.91), calls=%async_computation.6 | async-start | bytes 2097152 | tf_op jit(solution)/shard_map/all_to_all | solution.py:172
  280.8 20.8 %all-to-all-start.7 = ((bf16[64,16,512]{2,0,1:T(8,128)(2,1)}), bf16[64,16,512]{2,0,1:T(8,128)(2,1)}, u32[]{:S(2)}, u32[]{:S(2)}) async-start(bf16[64,16,512]{2,0,1:T(8,128)(2,1)} %copy.93), calls=%async_computation.7 | async-start | bytes 2097152 | tf_op jit(solution)/shard_map/all_to_all | solution.py:173
  301.6 21.1 %all-to-all-start.12 = ((bf16[64,16,512]{2,0,1:T(8,128)(2,1)}), bf16[64,16,512]{2,0,1:T(8,128)(2,1)}, u32[]{:S(2)}, u32[]{:S(2)}) async-start(bf16[64,16,512]{2,0,1:T(8,128)(2,1)} %copy.103), calls=%async_computation.12 | async-start | bytes 2097152 | tf_op jit(solution)/shard_map/all_to_all | solution.py:172
  322.7 20.8 %all-to-all-start.13 = ((bf16[64,16,512]{2,0,1:T(8,128)(2,1)}), bf16[64,16,512]{2,0,1:T(8,128)(2,1)}, u32[]{:S(2)}, u32[]{:S(2)}) async-start(bf16[64,16,512]{2,0,1:T(8,128)(2,1)} %copy.105), calls=%async_computation.13 | async-start | bytes 2097152 | tf_op jit(solution)/shard_map/all_to_all | solution.py:173
  343.6 20.8 %all-to-all-start.15 = ((bf16[64,16,512]{2,0,1:T(8,128)(2,1)}), bf16[64,16,512]{2,0,1:T(8,128)(2,1)}, u32[]{:S(2)}, u32[]{:S(2)}) async-start(bf16[64,16,512]{2,0,1:T(8,128)(2,1)} %copy.109), calls=%async_computation.15 | async-start | bytes 2097152 | tf_op jit(solution)/shard_map/all_to_all | solution.py:172
  350.6 17.9 %copy-start.16 = (u32[128]{0:T(128)S(1)}, u32[128]{0:T(128)}, u32[]{:S(2)}) copy-start(u32[128]{0:T(128)} %constant.110) | copy-start | bytes 1540
  364.4 24.5 %all-to-all-start.16 = ((bf16[64,16,512]{2,0,1:T(8,128)(2,1)}), bf16[64,16,512]{2,0,1:T(8,128)(2,1)S(1)}, u32[]{:S(2)}, u32[]{:S(2)}) async-start(bf16[64,16,512]{2,0,1:T(8,128)(2,1)} %copy.111), calls=%async_computation.16 | async-start | bytes 2097152 | tf_op jit(solution)/shard_map/all_to_all | solution.py:173
  388.9 25.0 %all-to-all-start.8 = ((bf16[16,32,512]{2,1,0:T(8,128)(2,1)}), bf16[16,32,512]{2,1,0:T(8,128)(2,1)S(1)}, u32[]{:S(2)}, u32[]{:S(2)}) async-start(bf16[16,32,512]{2,1,0:T(8,128)(2,1)} %bitcast.47), calls=%async_computation.8 | async-start | bytes 1048576 | tf_op jit(solution)/shard_map/all_to_all | solution.py:178
  413.9 23.8 %all-to-all-start.14 = ((bf16[16,32,512]{2,1,0:T(8,128)(2,1)}), bf16[16,32,512]{2,1,0:T(8,128)(2,1)S(1)}, u32[]{:S(2)}, u32[]{:S(2)}) async-start(bf16[16,32,512]{2,1,0:T(8,128)(2,1)} %bitcast.80), calls=%async_computation.14 | async-start | bytes 1048576 | tf_op jit(solution)/shard_map/all_to_all | solution.py:178
  437.6 18.8 %all-to-all-start.17 = ((bf16[16,32,512]{2,1,0:T(8,128)(2,1)}), bf16[16,32,512]{2,1,0:T(8,128)(2,1)}, u32[]{:S(2)}, u32[]{:S(2)}) async-start(bf16[16,32,512]{2,1,0:T(8,128)(2,1)} %bitcast.95), calls=%async_computation.17 | async-start | bytes 1048576 | tf_op jit(solution)/shard_map/all_to_all | solution.py:194
  443.4 105.8 %all-reduce.3.cloned.1.call-start = ((), (), s32[]{:S(2)}) async-start(), calls=%async_computation.18 | async-start | bytes 1048576
  458.4 2.9 copy-start.15
Sparse Core Ops, SparseCore 0:
  461.4 87.7 all-reduce.2
where the time goes:
time: 565 us; the launch traced here: 558 us
  waiting for transfers between devices  149 us (26%)
  local copies, waits for them, and re-layouts  104 us (18%)
  matrix products  96.4 us (17%)
  blocking collectives  79.9 us (14%)
  starting transfers between devices  69.3 us (12%)
  other arithmetic  44.2 us (8%)
  between operations  15.6 us (3%)
    unnamed x2, waiting for transfers between devices  84.6 us
    all_to_all x2, blocking collectives, spectrum_of(): lax.all_to_all(real_part, 'ctx', split_axis=0, concat_axis=2, tiled=True)  40.4 us
    all_to_all x2, blocking collectives, spectrum_of(): lax.all_to_all(imag_part, 'ctx', split_axis=0, concat_axis=2, tiled=True)  39.5 us
    all_to_all x3, waiting for transfers between devices, columns_of(): lax.all_to_all(real_part, 'ctx', split_axis=1, concat_axis=0, tiled=True)  33.4 us
    dot_general x3, matrix products, last_section(): jnp.dot(back_imag, imag_part.reshape(N1, item_count), preferred_element_t...  29.3 us
    dot_general x3, matrix products, last_section(): jnp.dot(back_real, real_part.reshape(N1, item_count), preferred_element_t...  27 us
    transpose x6, local copies, waits for them, and re-layouts, arrange(): jnp.transpose(part, (0, 2, 1))  24 us
    transpose x6, local copies, waits for them, and re-layouts, arrange(): moved = jnp.transpose(part.reshape(item_count, N2, chan_count), (0, 2, 1))  21.4 us
  transfers between devices with their start and end apart: 15, of which 9 were waited for; matrix products, arithmetic and copies ran while one was open for 32% of the time, Pallas kernels for 0%

commit v1 on v0

v1 whole, which is shorter than its diff:
```python
import math

import jax
import jax.numpy as jnp
import numpy as np
from jax import lax
from jax.sharding import PartitionSpec as P

N1 = 1024
N2 = 512
SEQ = 262144
HALF = N1 // 2
POINTS = N1 * N2


def tables():
    n1 = np.arange(HALF, dtype=np.int64)
    k1 = np.arange(HALF, dtype=np.int64)
    n2 = np.arange(N2, dtype=np.int64)
    ang_a = ((2 * k1 + 1)[:, None] * n1[None, :] % (2 * N1)) * (math.pi / N1)
    ang_b = (n2[:, None] * n2[None, :] % N2) * (2.0 * math.pi / N2)
    ang_t = ((2 * k1 + 1)[:, None] * n2[None, :] % (2 * POINTS)) * (math.pi / POINTS)
    first = np.concatenate([np.cos(ang_a), -np.sin(ang_a)], axis=0)
    cos_b, sin_b = np.cos(ang_b), np.sin(ang_b)
    second = np.block([[cos_b, -sin_b], [sin_b, cos_b]])
    back_second = np.block([[cos_b, sin_b], [-sin_b, cos_b]])
    back_first = 2.0 / POINTS * np.concatenate([np.cos(ang_a).T, -np.sin(ang_a).T], axis=1)
    half = lambda a: jnp.asarray(a.astype(np.float32)).astype(jnp.bfloat16)
    full = lambda a: jnp.asarray(a.astype(np.float32))
    return half(first), half(second), half(back_second), half(back_first), full(np.cos(ang_t)), full(np.sin(ang_t))


def body(signal, gate, cotangent, skip_gain, filter_taps):
    shards = lax.axis_size("ctx")
    channels = signal.shape[0]
    rows = signal.shape[1] // N2
    first, second, back_second, back_first, tw_cos, tw_sin = tables()

    def to_grid(values):
        blocks = values.reshape(channels, rows, N2)
        return lax.all_to_all(blocks, "ctx", split_axis=0, concat_axis=0, tiled=True).reshape(HALF, N2)

    def to_rows(grid):
        blocks = grid.astype(jnp.bfloat16).reshape(shards, rows, N2)
        return lax.all_to_all(blocks, "ctx", split_axis=0, concat_axis=0, tiled=True)

    def spectrum(grid):
        summed = jnp.dot(first, grid, preferred_element_type=jnp.float32)
        re, im = summed[:HALF], summed[HALF:]
        both = jnp.concatenate([re * tw_cos + im * tw_sin, im * tw_cos - re * tw_sin], axis=1)
        out = jnp.dot(both.astype(jnp.bfloat16), second, preferred_element_type=jnp.float32)
        return out[:, :N2], out[:, N2:]

    def invert(re, im):
        both = jnp.concatenate([re, im], axis=1).astype(jnp.bfloat16)
        out = jnp.dot(both, back_second, preferred_element_type=jnp.float32)
        re, im = out[:, :N2], out[:, N2:]
        stacked = jnp.concatenate([re * tw_cos - im * tw_sin, re * tw_sin + im * tw_cos], axis=0)
        return jnp.dot(back_first, stacked.astype(jnp.bfloat16), preferred_element_type=jnp.float32)

    def conj_product(a, b):
        return a[0] * b[0] + a[1] * b[1], a[1] * b[0] - a[0] * b[1]

    upstream = gate.astype(jnp.float32) * cotangent.astype(jnp.float32)
    spec_h = spectrum(to_grid(filter_taps.astype(jnp.bfloat16)))
    spec_x = spectrum(to_grid(signal))
    spec_u = spectrum(to_grid(upstream.astype(jnp.bfloat16)))
    product = spec_x[0] * spec_h[0] - spec_x[1] * spec_h[1], spec_x[0] * spec_h[1] + spec_x[1] * spec_h[0]
    conv = to_rows(invert(*product)).reshape(channels, rows * N2)
    taps = to_rows(invert(*conj_product(spec_u, spec_x)))
    corr = to_rows(invert(*conj_product(spec_u, spec_h))).reshape(channels, rows * N2)
    terms = lax.all_to_all(taps, "ch", split_axis=0, concat_axis=0, tiled=True)
    terms = terms.reshape(lax.axis_size("ch"), -1, rows, N2).astype(jnp.float32)
    grad_taps = (jnp.sum(terms, axis=0) / math.sqrt(SEQ)).reshape(-1, rows * N2)
    mixed = conv.astype(jnp.float32) + skip_gain[:, None] * signal.astype(jnp.float32)
    output = (gate.astype(jnp.float32) * mixed).astype(jnp.bfloat16)
    grad_gate = (cotangent.astype(jnp.float32) * mixed).astype(jnp.bfloat16)
    grad_signal = (corr.astype(jnp.float32) + skip_gain[:, None] * upstream).astype(jnp.bfloat16)
    return output, grad_gate, grad_signal, grad_taps


def solution(mesh):
    return jax.shard_map(
        body,
        mesh=mesh,
        in_specs=(P("ch", "ctx"), P("ch", "ctx"), P("ch", "ctx"), P("ch"), P(None, "ctx")),
        out_specs=(P("ch", "ctx"), P("ch", "ctx"), P("ch", "ctx"), P("ch", "ctx")),
        check_vma=False,
    )
```

time: 565 us -> 125 us (0.22)
  the two profiles are of different devices: /device:TPU:0 before, /device:TPU:1 now
where the time goes in v1:
time: 125 us; the launch traced here: 124 us
  starting transfers between devices  40.4 us (32%)
  waiting for transfers between devices  37.8 us (30%)
  matrix products  25.8 us (21%)
  local copies, waits for them, and re-layouts  13.2 us (11%)
  other arithmetic  5.56 us (4%)
    all_to_all x3, starting transfers between devices, to_grid(): lax.all_to_all(blocks, 'ctx', split_axis=0, concat_axis=0, tiled=True)  16.6 us
    all_to_all x3, starting transfers between devices, to_rows(): lax.all_to_all(blocks, 'ctx', split_axis=0, concat_axis=0, tiled=True)  16.6 us
    all_to_all x3, waiting for transfers between devices, to_grid(): lax.all_to_all(blocks, 'ctx', split_axis=0, concat_axis=0, tiled=True)  14.5 us
    all_to_all x3, waiting for transfers between devices, to_rows(): lax.all_to_all(blocks, 'ctx', split_axis=0, concat_axis=0, tiled=True)  14.4 us
    unnamed x56, local copies, waits for them, and re-layouts  13.2 us
    all_to_all x1, waiting for transfers between devices, body(): terms = lax.all_to_all(taps, 'ch', split_axis=0, concat_axis=0, tiled=True)  8.91 us
    dot_general x6, matrix products, invert(): jnp.dot(back_first, stacked.astype(jnp.bfloat16), preferred_element_type=...  7.43 us
    all_to_all x1, starting transfers between devices, body(): terms = lax.all_to_all(taps, 'ch', split_axis=0, concat_axis=0, tiled=True)  7.2 us
  transfers between devices with their start and end apart: 7, of which 5 were waited for; matrix products, arithmetic and copies ran while one was open for 27% of the time, Pallas kernels for 0%

profile of v1, /device:TPU:1, one launch (start us, length us, event | category | flops | bytes accessed | tf_op | source)
XLA Modules:
  0.0 123.7 jit_solution(2102555913213535026)
XLA Ops:
  0.6 1.3 %fusion.5 = bf16[16,16384]{1,0:T(8,128)(2,1)S(1)} fusion(bf16[16,16384]{1,0:T(8,128)(2,1)} %param.13, bf16[16,16384]{1,0:T(8,128)(2,1)} %param.12), kind=kLoop, calls=%fused_computation.38 | loop fusion | flops 1048576 | bytes 1572864 | tf_op jit(solution)/shard_map/convert_element_type | solution.py:67
  2.0 1.0 copy.18
  2.9 7.2 %all-to-all-start.3 = ((bf16[16,32,512]{2,1,0:T(8,128)(2,1)}), bf16[16,32,512]{2,1,0:T(8,128)(2,1)S(1)}, u32[]{:S(2)}, u32[]{:S(2)}) async-start(bf16[16,32,512]{2,1,0:T(8,128)(2,1)} %bitcast.21), calls=%async_computation.3 | async-start | bytes 1048576 | tf_op jit(solution)/shard_map/all_to_all | solution.py:41
  10.1 1.4 %convert_element_type.86 = bf16[16,16384]{1,0:T(8,128)(2,1)S(1)} convert(f32[16,16384]{1,0:T(8,128)} %param.15) | non-fusion elementwise | flops 262144 | bytes 1572864 | tf_op jit(solution)/shard_map/convert_element_type | solution.py:65
  11.5 1.0 copy.16
  12.4 7.5 %all-to-all-done.3 = bf16[16,32,512]{2,1,0:T(8,128)(2,1)S(1)} async-done(((bf16[16,32,512]{2,1,0:T(8,128)(2,1)}), bf16[16,32,512]{2,1,0:T(8,128)(2,1)S(1)}, u32[]{:S(2)}, u32[]{:S(2)}) %all-to-all-start.3) | async-done | bytes 524320 | tf_op jit(solution)/shard_map/all_to_all | solution.py:41
  20.0 4.4 %all-to-all-start.1 = ((bf16[16,32,512]{2,1,0:T(8,128)(2,1)}), bf16[16,32,512]{2,1,0:T(8,128)(2,1)S(1)}, u32[]{:S(2)}, u32[]{:S(2)}) async-start(bf16[16,32,512]{2,1,0:T(8,128)(2,1)} %bitcast.17), calls=%async_computation.1 | async-start | bytes 1048576 | tf_op jit(solution)/shard_map/all_to_all | solution.py:41
  24.4 1.0 copy.15
  25.4 2.1 %fusion.17 = f32[1024,512]{1,0:T(8,128)} fusion(bf16[1024,512]{1,0:T(8,128)(2,1)S(1)} %copy-done.9, bf16[512,512]{1,0:T(8,128)(2,1)S(1)} %bitcast.58), kind=kOutput, calls=%fused_computation.51 | convolution fusion | flops 536870912 | bytes 3670016 | tf_op jit(solution)/shard_map/dot_general | solution.py:48
  27.4 7.0 %all-to-all-done.1 = bf16[16,32,512]{2,1,0:T(8,128)(2,1)S(1)} async-done(((bf16[16,32,512]{2,1,0:T(8,128)(2,1)}), bf16[16,32,512]{2,1,0:T(8,128)(2,1)S(1)}, u32[]{:S(2)}, u32[]{:S(2)}) %all-to-all-start.1) | async-done | bytes 524320 | tf_op jit(solution)/shard_map/all_to_all | solution.py:41
  34.4 0.8 copy-done.21
  35.2 5.0 %all-to-all-start = ((bf16[16,32,512]{2,1,0:T(8,128)(2,1)}), bf16[16,32,512]{2,1,0:T(8,128)(2,1)}, u32[]{:S(2)}, u32[]{:S(2)}) async-start(bf16[16,32,512]{2,1,0:T(8,128)(2,1)} %bitcast.15), calls=%async_computation | async-start | bytes 1048576 | tf_op jit(solution)/shard_map/all_to_all | solution.py:41
  40.2 1.9 %fusion.16 = f32[1024,512]{1,0:T(8,128)S(1)} fusion(bf16[1024,512]{1,0:T(8,128)(2,1)S(1)} %copy-done.9, bf16[512,512]{1,0:T(8,128)(2,1)} %bitcast.59), kind=kOutput, calls=%fused_computation.50 | convolution fusion | flops 536870912 | bytes 3670016 | tf_op jit(solution)/shard_map/dot_general | solution.py:48
  42.2 2.3 %fusion.10 = f32[512,1024]{1,0:T(8,128)S(1)} fusion(bf16[512,1024]{1,0:T(8,128)(2,1)S(1)} %copy-done.10, f32[512,512]{1,0:T(8,128)S(1)} %copy-done.1, f32[512,512]{1,0:T(8,128)S(1)} %copy-done, f32[1024,512]{1,0:T(8,128)} %fusion.17), kind=kOutput, calls=%fused_computation.43 | convolution fusion | flops 537919488 | bytes 7340032 | tf_op jit(solution)/shard_map/dot_general | solution.py:51
  44.6 0.8 fusion.7
  45.8 0.7 copy-done.15
  46.5 0.8 convolution_add_fusion.2
  47.3 0.8 convolution_add_fusion.4
  48.1 1.2 copy-done.7
  49.3 0.8 fusion.11
  50.0 0.6 copy-done.4
  50.6 0.6 copy-done.6
  51.2 0.8 convolution_add_fusion.1
  52.3 0.5 fusion.12
  52.8 0.5 copy-done.16
  53.3 1.3 %fusion.1 = bf16[512,512]{0,1:T(8,128)(2,1)} fusion(f32[512,512]{0,1:T(8,128)S(1)} %fusion.12, bf16[512,512]{1,0:T(8,128)(2,1)S(1)} %copy-done.16, f32[512,512]{1,0:T(8,128)S(1)} %copy-done, f32[512,512]{1,0:T(8,128)S(1)} %copy-done.1, f32[512,1024]{1,0:T(8,128)S(1)} %convolution_add_fusion.1), kind=kOutput, calls=%fused_computation.13 | convolution fusion | flops 270008320 | bytes 6291456 | tf_op jit(solution)/shard_map/dot_general | solution.py:59
  54.7 5.8 %all-to-all-start.4 = ((bf16[16,32,512]{2,1,0:T(8,128)(2,1)}), bf16[16,32,512]{2,1,0:T(8,128)(2,1)}, u32[]{:S(2)}, u32[]{:S(2)}) async-start(bf16[16,32,512]{2,1,0:T(8,128)(2,1)} %bitcast.55), calls=%async_computation.4 | async-start | bytes 1048576 | tf_op jit(solution)/shard_map/all_to_all | solution.py:45
  60.5 2.2 %fusion.15 = f32[1024,512]{1,0:T(8,128)S(1)} fusion(bf16[1024,512]{1,0:T(8,128)(2,1)} %constant.23, bf16[512,512]{1,0:T(8,128)(2,1)} %bitcast), kind=kOutput, calls=%fused_computation.49 | convolution fusion | flops 536870912 | bytes 3670016 | tf_op jit(solution)/shard_map/dot_general | solution.py:48
  62.7 0.8 fusion.6
  63.9 0.8 convolution_add_fusion.5
  64.6 0.8 copy-done.5
  65.7 0.8 fusion.8
  66.5 0.8 convolution_add_fusion.3
  67.5 0.5 fusion.9
  68.6 1.3 %fusion = bf16[512,512]{0,1:T(8,128)(2,1)} fusion(f32[512,512]{0,1:T(8,128)S(1)} %fusion.9, bf16[512,512]{1,0:T(8,128)(2,1)S(1)} %copy-done.17, f32[512,512]{1,0:T(8,128)S(1)} %copy-done, f32[512,512]{1,0:T(8,128)S(1)} %copy-done.1, f32[512,1024]{1,0:T(8,128)S(1)} %convolution_add_fusion.3), kind=kOutput, calls=%fused_computation.12 | convolution fusion | flops 270008320 | bytes 6291456 | tf_op jit(solution)/shard_map/dot_general | solution.py:59
  70.3 0.8 fusion.13
  71.1 2.1 %convolution_add_fusion = f32[512,1024]{1,0:T(8,128)} fusion(f32[512,1024]{1,0:T(8,128)S(1)} %fusion.13, bf16[512,1024]{1,0:T(8,128)(2,1)S(1)} %copy-done.6, f32[512,1024]{1,0:T(8,128)S(1)} %copy-done.3, f32[512,1024]{1,0:T(8,128)S(1)} %convolution_add_fusion.5), kind=kOutput, calls=%fused_computation | convolution fusion | flops 538443776 | bytes 9437184 | tf_op jit(solution)/shard_map/dot_general | solution.py:56
  73.2 5.7 %all-to-all-start.2 = ((bf16[16,32,512]{2,1,0:T(8,128)(2,1)}), bf16[16,32,512]{2,1,0:T(8,128)(2,1)S(1)}, u32[]{:S(2)}, u32[]{:S(2)}) async-start(bf16[16,32,512]{2,1,0:T(8,128)(2,1)} %bitcast.56), calls=%async_computation.2 | async-start | bytes 1048576 | tf_op jit(solution)/shard_map/all_to_all | solution.py:45
  79.0 2.4 %fusion.14 = f32[512,512]{0,1:T(8,128)S(1)} fusion(bf16[512,512]{1,0:T(8,128)(2,1)} %constant.33, f32[512,512]{1,0:T(8,128)S(1)} %copy-done.1, f32[512,512]{1,0:T(8,128)S(1)} %copy-done, f32[512,1024]{1,0:T(8,128)} %convolution_add_fusion), kind=kOutput, calls=%fused_computation.47 | convolution fusion | flops 269484032 | bytes 5767168 | tf_op jit(solution)/shard_map/dot_general | solution.py:59
  81.4 1.3 %fusion.2 = bf16[512,512]{0,1:T(8,128)(2,1)} fusion(f32[512,512]{0,1:T(8,128)S(1)} %fusion.14, bf16[512,512]{1,0:T(8,128)(2,1)S(1)} %copy-done.18, f32[512,512]{1,0:T(8,128)S(1)} %copy-done, f32[512,512]{1,0:T(8,128)S(1)} %copy-done.1, f32[512,1024]{1,0:T(8,128)S(1)} %copy-done.14), kind=kOutput, calls=%fused_computation.14 | convolution fusion | flops 270008320 | bytes 6291456 | tf_op jit(solution)/shard_map/dot_general | solution.py:59
  82.8 6.1 %all-to-all-done.2 = bf16[16,32,512]{2,1,0:T(8,128)(2,1)S(1)} async-done(((bf16[16,32,512]{2,1,0:T(8,128)(2,1)}), bf16[16,32,512]{2,1,0:T(8,128)(2,1)S(1)}, u32[]{:S(2)}, u32[]{:S(2)}) %all-to-all-start.2) | async-done | bytes 524320 | tf_op jit(solution)/shard_map/all_to_all | solution.py:45
  88.9 5.0 %all-to-all-start.5 = ((bf16[16,32,512]{2,1,0:T(8,128)(2,1)}), bf16[16,32,512]{2,1,0:T(8,128)(2,1)}, u32[]{:S(2)}, u32[]{:S(2)}) async-start(bf16[16,32,512]{2,1,0:T(8,128)(2,1)} %bitcast.8), calls=%async_computation.5 | async-start | bytes 1048576 | tf_op jit(solution)/shard_map/all_to_all | solution.py:45
  93.9 1.4 %copy.19 = f32[2,8,32,512]{3,1,2,0:T(8,128)S(1)} copy(bf16[2,8,32,512]{3,2,1,0:T(8,128)(2,1)} %bitcast.28) | data formatting | bytes 1572864
  95.6 8.3 %all-to-all-done.5 = bf16[16,32,512]{2,1,0:T(8,128)(2,1)} async-done(((bf16[16,32,512]{2,1,0:T(8,128)(2,1)}), bf16[16,32,512]{2,1,0:T(8,128)(2,1)}, u32[]{:S(2)}, u32[]{:S(2)}) %all-to-all-start.5) | async-done | bytes 524320 | tf_op jit(solution)/shard_map/all_to_all | solution.py:45
  104.0 7.2 %all-to-all-start.6 = ((bf16[16,32,512]{2,1,0:T(8,128)(2,1)}), bf16[16,32,512]{2,1,0:T(8,128)(2,1)S(1)}, u32[]{:S(2)}, u32[]{:S(2)}) async-start(bf16[16,32,512]{2,1,0:T(8,128)(2,1)} %all-to-all-done.5), calls=%async_computation.6 | async-start | bytes 1048576 | tf_op jit(solution)/shard_map/all_to_all | solution.py:72
  111.2 2.8 %fusion.4 = (bf16[16,16384]{1,0:T(8,128)(2,1)}, bf16[16,16384]{1,0:T(8,128)(2,1)}, bf16[16,16384]{1,0:T(8,128)(2,1)}) fusion(bf16[16,16384]{1,0:T(8,128)(2,1)S(1)} %copy-done.22, f32[16,16384]{1,0:T(8,128)S(1)} %bitcast.54, bf16[16,16384]{1,0:T(8,128)(2,1)} %param.11, f32[16]{0:T(128)S(1)} %copy-done.24, bf16[16,16384]{1,0:T(8,128)(2,1)} %param.12, ...), kind=kLoop, calls=%fused_computation.16 | loop fusion | flops 3407872 | bytes 5242944 | tf_op jit(solution)/shard_map/convert_element_type | solution.py:77
  114.0 8.9 %all-to-all-done.6 = bf16[16,32,512]{2,1,0:T(8,128)(2,1)S(1)} async-done(((bf16[16,32,512]{2,1,0:T(8,128)(2,1)}), bf16[16,32,512]{2,1,0:T(8,128)(2,1)S(1)}, u32[]{:S(2)}, u32[]{:S(2)}) %all-to-all-start.6) | async-done | bytes 524320 | tf_op jit(solution)/shard_map/all_to_all | solution.py:72
  123.0 0.8 copy.20
  (48 shorter events, 3.1 us)
Async XLA Ops:
  2.9 17.1 %all-to-all-start.3 = ((bf16[16,32,512]{2,1,0:T(8,128)(2,1)}), bf16[16,32,512]{2,1,0:T(8,128)(2,1)S(1)}, u32[]{:S(2)}, u32[]{:S(2)}) async-start(bf16[16,32,512]{2,1,0:T(8,128)(2,1)} %bitcast.21), calls=%async_computation.3 | async-start | bytes 1048576 | tf_op jit(solution)/shard_map/all_to_all | solution.py:41
  10.1 14.3 %copy-start.23 = (bf16[16,16384]{1,0:T(8,128)(2,1)S(1)}, bf16[16,16384]{1,0:T(8,128)(2,1)}, u32[]{:S(2)}) copy-start(bf16[16,16384]{1,0:T(8,128)(2,1)} %param.11) | copy-start | bytes 1572868
  10.1 15.3 %copy-start.9 = (bf16[1024,512]{1,0:T(8,128)(2,1)S(1)}, bf16[1024,512]{1,0:T(8,128)(2,1)}, u32[]{:S(2)}) copy-start(bf16[1024,512]{1,0:T(8,128)(2,1)} %constant.23) | copy-start | bytes 3145732
  20.0 14.4 %all-to-all-start.1 = ((bf16[16,32,512]{2,1,0:T(8,128)(2,1)}), bf16[16,32,512]{2,1,0:T(8,128)(2,1)S(1)}, u32[]{:S(2)}, u32[]{:S(2)}) async-start(bf16[16,32,512]{2,1,0:T(8,128)(2,1)} %bitcast.17), calls=%async_computation.1 | async-start | bytes 1048576 | tf_op jit(solution)/shard_map/all_to_all | solution.py:41
  34.4 0.8 copy-start.21
  35.2 19.5 %all-to-all-start = ((bf16[16,32,512]{2,1,0:T(8,128)(2,1)}), bf16[16,32,512]{2,1,0:T(8,128)(2,1)}, u32[]{:S(2)}, u32[]{:S(2)}) async-start(bf16[16,32,512]{2,1,0:T(8,128)(2,1)} %bitcast.15), calls=%async_computation | async-start | bytes 1048576 | tf_op jit(solution)/shard_map/all_to_all | solution.py:41
  40.2 1.9 %copy-start = (f32[512,512]{1,0:T(8,128)S(1)}, f32[512,512]{1,0:T(8,128)}, u32[]{:S(2)}) copy-start(f32[512,512]{1,0:T(8,128)} %constant.21.clone) | copy-start | bytes 3145732
  40.2 1.9 %copy-start.1 = (f32[512,512]{1,0:T(8,128)S(1)}, f32[512,512]{1,0:T(8,128)}, u32[]{:S(2)}) copy-start(f32[512,512]{1,0:T(8,128)} %constant.22.clone) | copy-start | bytes 3145732
  40.2 2.0 %copy-start.10 = (bf16[512,1024]{1,0:T(8,128)(2,1)S(1)}, bf16[512,1024]{1,0:T(8,128)(2,1)}, u32[]{:S(2)}) copy-start(bf16[512,1024]{1,0:T(8,128)(2,1)} %constant.27) | copy-start | bytes 3145732
  44.5 1.2 copy-start.12
  44.6 1.9 %copy-start.15 = (f32[1024,512]{1,0:T(8,128)S(1)}, f32[1024,512]{1,0:T(8,128)}, u32[]{:S(2)}) copy-start(f32[1024,512]{1,0:T(8,128)} %fusion.17) | copy-start | bytes 6291460
  47.3 2.8 %copy-start.2 = (f32[512,1024]{1,0:T(8,128)}, f32[512,1024]{1,0:T(8,128)S(1)}, u32[]{:S(2)}) copy-start(f32[512,1024]{1,0:T(8,128)S(1)} %convolution_add_fusion.2) | copy-start | bytes 6291460
  47.3 2.0 %copy-start.7 = (bf16[512,1024]{1,0:T(8,128)(2,1)S(1)}, bf16[512,1024]{1,0:T(8,128)(2,1)}, u32[]{:S(2)}) copy-start(bf16[512,1024]{1,0:T(8,128)(2,1)} %constant.31) | copy-start | bytes 3145732
  49.3 1.3 %copy-start.4 = (f32[512,1024]{1,0:T(8,128)}, f32[512,1024]{1,0:T(8,128)S(1)}, u32[]{:S(2)}) copy-start(f32[512,1024]{1,0:T(8,128)S(1)} %convolution_add_fusion.4) | copy-start | bytes 6291460
  49.3 2.0 %copy-start.6 = (bf16[512,1024]{1,0:T(8,128)(2,1)S(1)}, bf16[512,1024]{1,0:T(8,128)(2,1)}, u32[]{:S(2)}) copy-start(bf16[512,1024]{1,0:T(8,128)(2,1)} %constant.32) | copy-start | bytes 3145732
  51.2 1.0 copy-start.19
  52.3 1.0 copy-start.16
  54.7 18.6 %all-to-all-start.4 = ((bf16[16,32,512]{2,1,0:T(8,128)(2,1)}), bf16[16,32,512]{2,1,0:T(8,128)(2,1)}, u32[]{:S(2)}, u32[]{:S(2)}) async-start(bf16[16,32,512]{2,1,0:T(8,128)(2,1)} %bitcast.55), calls=%async_computation.4 | async-start | bytes 1048576 | tf_op jit(solution)/shard_map/all_to_all | solution.py:45
  60.5 2.2 %copy-start.11 = (bf16[512,1024]{1,0:T(8,128)(2,1)S(1)}, bf16[512,1024]{1,0:T(8,128)(2,1)}, u32[]{:S(2)}) copy-start(bf16[512,1024]{1,0:T(8,128)(2,1)} %constant.27) | copy-start | bytes 3145732
  62.6 1.2 copy-start.13
  63.9 1.6 %copy-start.5 = (f32[512,1024]{1,0:T(8,128)S(1)}, f32[512,1024]{1,0:T(8,128)}, u32[]{:S(2)}) copy-start(f32[512,1024]{1,0:T(8,128)} %copy-done.4) | copy-start | bytes 6291460
  63.9 1.9 %copy-start.8 = (bf16[512,1024]{1,0:T(8,128)(2,1)S(1)}, bf16[512,1024]{1,0:T(8,128)(2,1)}, u32[]{:S(2)}) copy-start(bf16[512,1024]{1,0:T(8,128)(2,1)} %constant.31) | copy-start | bytes 3145732
  66.5 1.0 copy-start.20
  67.5 1.0 copy-start.17
  68.6 1.8 %copy-start.3 = (f32[512,1024]{1,0:T(8,128)S(1)}, f32[512,1024]{1,0:T(8,128)}, u32[]{:S(2)}) copy-start(f32[512,1024]{1,0:T(8,128)} %copy-done.2) | copy-start | bytes 6291460
  73.2 15.6 %all-to-all-start.2 = ((bf16[16,32,512]{2,1,0:T(8,128)(2,1)}), bf16[16,32,512]{2,1,0:T(8,128)(2,1)S(1)}, u32[]{:S(2)}, u32[]{:S(2)}) async-start(bf16[16,32,512]{2,1,0:T(8,128)(2,1)} %bitcast.56), calls=%async_computation.2 | async-start | bytes 1048576 | tf_op jit(solution)/shard_map/all_to_all | solution.py:45
  79.0 2.4 %copy-start.14 = (f32[512,1024]{1,0:T(8,128)S(1)}, f32[512,1024]{1,0:T(8,128)}, u32[]{:S(2)}) copy-start(f32[512,1024]{1,0:T(8,128)} %convolution_add_fusion) | copy-start | bytes 6291460
  79.0 2.5 %copy-start.18 = (bf16[512,512]{1,0:T(8,128)(2,1)S(1)}, bf16[512,512]{1,0:T(8,128)(2,1)}, u32[]{:S(2)}) copy-start(bf16[512,512]{1,0:T(8,128)(2,1)} %constant.34) | copy-start | bytes 1572868
  88.9 15.1 %all-to-all-start.5 = ((bf16[16,32,512]{2,1,0:T(8,128)(2,1)}), bf16[16,32,512]{2,1,0:T(8,128)(2,1)}, u32[]{:S(2)}, u32[]{:S(2)}) async-start(bf16[16,32,512]{2,1,0:T(8,128)(2,1)} %bitcast.8), calls=%async_computation.5 | async-start | bytes 1048576 | tf_op jit(solution)/shard_map/all_to_all | solution.py:45
  93.9 17.3 %copy-start.22 = (bf16[16,16384]{1,0:T(8,128)(2,1)S(1)}, bf16[16,16384]{1,0:T(8,128)(2,1)}, u32[]{:S(2)}) copy-start(bf16[16,16384]{1,0:T(8,128)(2,1)} %param.13) | copy-start | bytes 1572868
  93.9 17.3 %copy-start.24 = (f32[16]{0:T(128)S(1)}, f32[16]{0:T(128)}, u32[]{:S(2)}) copy-start(f32[16]{0:T(128)} %param.14) | copy-start | bytes 196
  104.0 18.9 %all-to-all-start.6 = ((bf16[16,32,512]{2,1,0:T(8,128)(2,1)}), bf16[16,32,512]{2,1,0:T(8,128)(2,1)S(1)}, u32[]{:S(2)}, u32[]{:S(2)}) async-start(bf16[16,32,512]{2,1,0:T(8,128)(2,1)} %all-to-all-done.5), calls=%async_computation.6 | async-start | bytes 1048576 | tf_op jit(solution)/shard_map/all_to_all | solution.py:72

commit v2 on v1

v2 whole, which is shorter than its diff:
```python
import functools
import math

import jax
import jax.numpy as jnp
import numpy as np
from jax import lax
from jax.experimental import pallas as pl
from jax.experimental.pallas import tpu as pltpu
from jax.sharding import PartitionSpec as P

N1 = 1024
N2 = 512
SEQ = 262144
HALF = N1 // 2
POINTS = N1 * N2
MESH = pl.DeviceIdType.MESH


def tables():
    n1 = np.arange(HALF, dtype=np.int64)
    k1 = np.arange(HALF, dtype=np.int64)
    n2 = np.arange(N2, dtype=np.int64)
    ang_a = ((2 * k1 + 1)[:, None] * n1[None, :] % (2 * N1)) * (math.pi / N1)
    ang_b = (n2[:, None] * n2[None, :] % N2) * (2.0 * math.pi / N2)
    ang_t = ((2 * k1 + 1)[:, None] * n2[None, :] % (2 * POINTS)) * (math.pi / POINTS)
    first = np.concatenate([np.cos(ang_a), -np.sin(ang_a)], axis=0)
    cos_b, sin_b = np.cos(ang_b), np.sin(ang_b)
    second = np.concatenate([cos_b, sin_b, cos_b, -sin_b, cos_b], axis=0)
    back_first = 2.0 / POINTS * np.concatenate([np.cos(ang_a).T, -np.sin(ang_a).T], axis=1)
    half = lambda a: jnp.asarray(a.astype(np.float32)).astype(jnp.bfloat16)
    full = lambda a: jnp.asarray(a.astype(np.float32))
    return half(first), half(second), half(back_first), full(np.cos(ang_t)), full(np.sin(ang_t))


def dot(a, b):
    return jnp.dot(a, b, preferred_element_type=jnp.float32)


def kernel(
    shards, chs, rows, block,
    sig_hbm, gate_hbm, cot_hbm, skip_ref, taps_hbm, first_hbm, second_hbm, back_hbm, twc_hbm, tws_hbm,
    out_ref, ggate_ref, gsig_ref, gtaps_ref,
    sig, gate, cot, taps, first, second, back, twc, tws,
    flat, send, recv, spec, both, stack, ysend, yrecv,
    load_sem, send_sem, recv_sem,
):
    me = lax.axis_index("ctx")
    ch = lax.axis_index("ch")
    own = shards // chs

    loads = [
        pltpu.make_async_copy(src, dst, load_sem.at[i])
        for i, (src, dst) in enumerate(
            [(sig_hbm, sig), (taps_hbm, taps), (gate_hbm, gate), (cot_hbm, cot), (first_hbm, first),
             (twc_hbm, twc), (tws_hbm, tws), (second_hbm, second), (back_hbm, back)]
        )
    ]
    for load in loads:
        load.start()

    barrier = pltpu.get_barrier_semaphore()

    def greet_ctx(step, carry):
        pl.semaphore_signal(barrier, inc=1, device_id={"ctx": lax.rem(me + step, shards)}, device_id_type=MESH)
        return carry

    lax.fori_loop(1, shards, greet_ctx, 0)

    def is_self(peer_ctx, peer_ch):
        return jnp.logical_and(peer_ctx == me, peer_ch == ch)

    def greet_owners(at, carry):
        peer_ctx, peer_ch = own * ch + lax.rem(at, own), at // own

        @pl.when(jnp.logical_not(is_self(peer_ctx, peer_ch)))
        def _():
            pl.semaphore_signal(
                barrier, inc=1, device_id={"ctx": peer_ctx, "ch": peer_ch}, device_id_type=MESH
            )

        return carry

    lax.fori_loop(0, shards, greet_owners, 0)

    def spread(which, value_at):
        def one(row, carry):
            for lane in range(N2 // 128):
                cols = pl.ds(pl.multiple_of(row * N2 + lane * 128, 128), 128)
                flat[lane, pl.ds(row, shards, stride=rows), :] = value_at(cols)
            return carry

        lax.fori_loop(0, rows, one, 0)

        def cast(at, carry):
            here = pl.ds(pl.multiple_of(at * rows, rows), rows)
            for lane in range(N2 // 128):
                send[which, at, :, lane * 128 : (lane + 1) * 128] = flat[lane, here, :].astype(jnp.bfloat16)
            return carry

        lax.fori_loop(0, shards, cast, 0)

    def remote(src, dst, which, slot_out, slot_in, device):
        return pltpu.make_async_remote_copy(
            src_ref=src, dst_ref=dst, send_sem=send_sem.at[which, slot_out], recv_sem=recv_sem.at[which, slot_in],
            device_id=device, device_id_type=MESH,
        )

    def exchange(which, src, dst):
        def one(step, carry):
            peer = lax.rem(me + step, shards)
            remote(src.at[peer], dst.at[me], which, peer, me, {"ctx": peer}).start()
            return carry

        pltpu.make_async_copy(src.at[me], dst.at[me], recv_sem.at[which, me]).start()
        lax.fori_loop(1, shards, one, 0)

    def arrive(which, src, dst):
        pltpu.make_async_copy(src.at[me], dst.at[me], recv_sem.at[which, me]).wait()

        def one(step, carry):
            peer = lax.rem(me + shards - step, shards)
            remote(src.at[peer], dst.at[peer], which, peer, peer, {"ctx": peer}).wait_recv()
            return carry

        lax.fori_loop(1, shards, one, 0)

    def drain(which, src, dst):
        def one(step, carry):
            peer = lax.rem(me + step, shards)
            remote(src.at[peer], dst.at[me], which, peer, me, {"ctx": peer}).wait_send()
            return carry

        lax.fori_loop(1, shards, one, 0)

    def twist(at):
        here = pl.ds(pl.multiple_of(at * block, block), block)
        return here, twc[here, :], tws[here, :]

    def forward(which):
        def one(at, carry):
            here, cos, sin = twist(at)
            grid = recv[which].reshape(HALF, N2)
            re = dot(first[here, :], grid)
            im = dot(first[pl.ds(pl.multiple_of(HALF + at * block, block), block), :], grid)
            both[:, :N2] = (re * cos + im * sin).astype(jnp.bfloat16)
            both[:, N2:] = (im * cos - re * sin).astype(jnp.bfloat16)
            spec[which, 0, here, :] = dot(both[...], second[: 2 * N2, :])
            spec[which, 1, here, :] = dot(both[...], second[3 * N2 :, :])
            return carry

        lax.fori_loop(0, HALF // block, one, 0)

    def inverse(slot, left, right, conj):
        def one(at, carry):
            here, cos, sin = twist(at)
            l_re, l_im = spec[left, 0, here, :], spec[left, 1, here, :]
            r_re, r_im = spec[right, 0, here, :], spec[right, 1, here, :]
            if conj:
                re, im = l_re * r_re + l_im * r_im, l_im * r_re - l_re * r_im
            else:
                re, im = l_re * r_re - l_im * r_im, l_re * r_im + l_im * r_re
            both[:, :N2] = re.astype(jnp.bfloat16)
            both[:, N2:] = im.astype(jnp.bfloat16)
            re = dot(both[...], second[2 * N2 : 4 * N2, :])
            im = dot(both[...], second[N2 : 3 * N2, :])
            stack[here, :] = (re * cos - im * sin).astype(jnp.bfloat16)
            stack[pl.ds(pl.multiple_of(HALF + at * block, block), block), :] = (re * sin + im * cos).astype(
                jnp.bfloat16
            )
            return carry

        lax.fori_loop(0, HALF // block, one, 0)

        def last(at, carry):
            here = pl.ds(pl.multiple_of(at * block, block), block)
            value = dot(back[here, :], stack[...]).astype(jnp.bfloat16)
            ysend[slot, pl.ds(at * (block // rows), block // rows)] = value.reshape(block // rows, rows, N2)
            return carry

        lax.fori_loop(0, HALF // block, last, 0)

    loads[0].wait()
    spread(0, lambda cols: sig[:, cols].astype(jnp.float32))
    pl.semaphore_wait(barrier, 2 * shards - 1 - jnp.where(me // own == ch, 1, 0))
    exchange(0, send.at[0], recv.at[0])
    loads[1].wait()
    spread(1, lambda cols: taps[:, cols])
    exchange(1, send.at[1], recv.at[1])
    loads[2].wait()
    loads[3].wait()
    spread(2, lambda cols: gate[:, cols].astype(jnp.float32) * cot[:, cols].astype(jnp.float32))
    exchange(2, send.at[2], recv.at[2])
    for load in loads[4:]:
        load.wait()
    arrive(0, send.at[0], recv.at[0])
    forward(0)
    arrive(1, send.at[1], recv.at[1])
    forward(1)
    inverse(0, 0, 1, False)
    exchange(3, ysend.at[0], yrecv.at[0])
    arrive(2, send.at[2], recv.at[2])
    forward(2)
    inverse(1, 2, 1, True)
    exchange(4, ysend.at[1], yrecv.at[1])
    inverse(2, 2, 0, True)

    mine = lax.rem(me, own) + own * ch
    owner = me // own

    def give(step, wait):
        peer = lax.rem(me + step, shards)
        local = is_self(peer, owner)

        @pl.when(local)
        def _():
            copy = pltpu.make_async_copy(ysend.at[2, peer], yrecv.at[2, mine], recv_sem.at[5, mine])
            copy.wait() if wait else copy.start()

        @pl.when(jnp.logical_not(local))
        def _():
            copy = remote(ysend.at[2, peer], yrecv.at[2, mine], 5, peer, mine, {"ctx": peer, "ch": owner})
            copy.wait_send() if wait else copy.start()

    def give_start(step, carry):
        give(step, False)
        return carry

    def give_wait(step, carry):
        give(step, True)
        return carry

    def take(at, carry):
        peer_ctx, peer_ch = own * ch + lax.rem(at, own), at // own

        @pl.when(jnp.logical_not(is_self(peer_ctx, peer_ch)))
        def _():
            remote(
                ysend.at[2, 0], yrecv.at[2, at], 5, 0, at, {"ctx": peer_ctx, "ch": peer_ch}
            ).wait_recv()

        return carry

    lax.fori_loop(0, shards, give_start, 0)

    def gather(slot):
        def one(at, carry):
            here = pl.ds(pl.multiple_of(at * rows, rows), rows)
            for lane in range(N2 // 128):
                flat[lane, here, :] = yrecv[slot, at, :, lane * 128 : (lane + 1) * 128].astype(jnp.float32)
            return carry

        lax.fori_loop(0, shards, one, 0)

    skip = skip_ref[...]
    arrive(3, ysend.at[0], yrecv.at[0])
    gather(0)

    def finish_conv(row, carry):
        for lane in range(N2 // 128):
            cols = pl.ds(pl.multiple_of(row * N2 + lane * 128, 128), 128)
            mixed = flat[lane, pl.ds(row, shards, stride=rows), :] + skip * sig[:, cols].astype(jnp.float32)
            out_ref[:, cols] = (gate[:, cols].astype(jnp.float32) * mixed).astype(jnp.bfloat16)
            ggate_ref[:, cols] = (cot[:, cols].astype(jnp.float32) * mixed).astype(jnp.bfloat16)
        return carry

    lax.fori_loop(0, rows, finish_conv, 0)
    arrive(4, ysend.at[1], yrecv.at[1])
    gather(1)

    def finish_corr(row, carry):
        for lane in range(N2 // 128):
            cols = pl.ds(pl.multiple_of(row * N2 + lane * 128, 128), 128)
            upstream = gate[:, cols].astype(jnp.float32) * cot[:, cols].astype(jnp.float32)
            corr = flat[lane, pl.ds(row, shards, stride=rows), :]
            gsig_ref[:, cols] = (corr + skip * upstream).astype(jnp.bfloat16)
        return carry

    lax.fori_loop(0, rows, finish_corr, 0)
    lax.fori_loop(0, shards, give_wait, 0)
    lax.fori_loop(0, shards, take, 0)
    scale = 1.0 / math.sqrt(SEQ)
    for group in range(own):
        total = yrecv[2, group].astype(jnp.float32)
        for at in range(1, chs):
            total = total + yrecv[2, own * at + group].astype(jnp.float32)
        for lane in range(N2 // 128):
            flat[lane, group * rows : (group + 1) * rows, :] = total[:, lane * 128 : (lane + 1) * 128] * scale

    def finish_taps(row, carry):
        for lane in range(N2 // 128):
            cols = pl.ds(pl.multiple_of(row * N2 + lane * 128, 128), 128)
            gtaps_ref[:, cols] = flat[lane, pl.ds(row, own, stride=rows), :]
        return carry

    lax.fori_loop(0, rows, finish_taps, 0)
    for which in range(3):
        drain(which, send.at[which], recv.at[which])
    drain(3, ysend.at[0], yrecv.at[0])
    drain(4, ysend.at[1], yrecv.at[1])


def body(shards, chs, signal, gate, cotangent, skip_gain, filter_taps):
    channels, positions = signal.shape
    rows = positions // N2
    own = shards // chs
    block = 256
    bf16, f32 = jnp.bfloat16, jnp.float32
    hbm = pl.BlockSpec(memory_space=pl.ANY)
    vmem = pl.BlockSpec(memory_space=pltpu.VMEM)
    return pl.pallas_call(
        functools.partial(kernel, shards, chs, rows, block),
        out_shape=[jax.ShapeDtypeStruct((channels, positions), bf16)] * 3
        + [jax.ShapeDtypeStruct((own, positions), f32)],
        in_specs=[hbm] * 3 + [vmem] + [hbm] * 6,
        out_specs=[vmem] * 4,
        scratch_shapes=[
            pltpu.VMEM((channels, positions), bf16),
            pltpu.VMEM((channels, positions), bf16),
            pltpu.VMEM((channels, positions), bf16),
            pltpu.VMEM((channels, positions), f32),
            pltpu.VMEM((2 * HALF, HALF), bf16),
            pltpu.VMEM((5 * N2, N2), bf16),
            pltpu.VMEM((HALF, 2 * HALF), bf16),
            pltpu.VMEM((HALF, N2), f32),
            pltpu.VMEM((HALF, N2), f32),
            pltpu.VMEM((N2 // 128, HALF, 128), f32),
            pltpu.VMEM((3, shards, rows, N2), bf16),
            pltpu.VMEM((3, shards, rows, N2), bf16),
            pltpu.VMEM((3, 2, HALF, N2), f32),
            pltpu.VMEM((block, 2 * N2), bf16),
            pltpu.VMEM((2 * HALF, N2), bf16),
            pltpu.VMEM((3, shards, rows, N2), bf16),
            pltpu.VMEM((3, shards, rows, N2), bf16),
            pltpu.SemaphoreType.DMA((9,)),
            pltpu.SemaphoreType.DMA((6, shards)),
            pltpu.SemaphoreType.DMA((6, shards)),
        ],
        compiler_params=pltpu.CompilerParams(
            collective_id=0, has_side_effects=True, vmem_limit_bytes=48 * 1024 * 1024
        ),
    )(signal, gate, cotangent, skip_gain.reshape(channels, 1), filter_taps, *tables())


def solution(mesh):
    return jax.shard_map(
        functools.partial(body, mesh.shape["ctx"], mesh.shape["ch"]),
        mesh=mesh,
        in_specs=(P("ch", "ctx"), P("ch", "ctx"), P("ch", "ctx"), P("ch"), P(None, "ctx")),
        out_specs=(P("ch", "ctx"), P("ch", "ctx"), P("ch", "ctx"), P("ch", "ctx")),
        check_vma=False,
    )
```

time: 125 us -> 64.5 us (0.52)
  the two profiles are of different devices: /device:TPU:1 before, /device:TPU:17 now
where the time goes in v2:
time: 64.5 us; the launch traced here: 64.2 us
  Pallas kernels  54.2 us (84%)
  local copies, waits for them, and re-layouts  9.34 us (14%)
  between operations  0.65 us (1%)
    pallas_call x1, Pallas kernels, body(): pl.pallas_call(functools.partial(kernel, shards, chs, rows, block), out_s...  54.2 us
    unnamed x14, local copies, waits for them, and re-layouts  8.61 us

profile of v2, /device:TPU:17, one launch (start us, length us, event | category | flops | bytes accessed | tf_op | source)
XLA Modules:
  0.0 64.2 jit_solution(3957193569043211546)
XLA Ops:
  0.6 0.7 %copy.14.skip_ref = f32[16,1]{1,0:T(8,128)S(1)} copy(f32[16,1]{0,1:T(1,128)} %bitcast.1) | data formatting | bytes 128 | tf_op jit(solution)/shard_map/reshape | solution.py:342
  1.4 0.0 copy-start
  1.4 1.2 %copy-done = f32[16,16384]{1,0:T(8,128)S(1)} copy-done((f32[16,16384]{1,0:T(8,128)S(1)}, f32[16,16384]{1,0:T(8,128)}, u32[]{:S(2)}) %copy-start) | copy-done | bytes 1048600
  2.6 0.0 copy-start.1
  2.6 1.2 %copy-done.1 = bf16[1024,512]{1,0:T(8,128)(2,1)S(1)} copy-done((bf16[1024,512]{1,0:T(8,128)(2,1)S(1)}, bf16[1024,512]{1,0:T(8,128)(2,1)}, u32[]{:S(2)}) %copy-start.1) | copy-done | bytes 1048600
  3.8 0.0 copy-start.2
  3.8 1.0 %copy-done.2 = bf16[16,16384]{1,0:T(8,128)(2,1)S(1)} copy-done((bf16[16,16384]{1,0:T(8,128)(2,1)S(1)}, bf16[16,16384]{1,0:T(8,128)(2,1)}, u32[]{:S(2)}) %copy-start.2) | copy-done | bytes 524312
  4.9 0.0 copy-start.3
  4.9 1.0 %copy-done.3 = bf16[16,16384]{1,0:T(8,128)(2,1)S(1)} copy-done((bf16[16,16384]{1,0:T(8,128)(2,1)S(1)}, bf16[16,16384]{1,0:T(8,128)(2,1)}, u32[]{:S(2)}) %copy-start.3) | copy-done | bytes 524312
  5.9 0.0 copy-start.4
  5.9 1.0 %copy-done.4 = bf16[16,16384]{1,0:T(8,128)(2,1)S(1)} copy-done((bf16[16,16384]{1,0:T(8,128)(2,1)S(1)}, bf16[16,16384]{1,0:T(8,128)(2,1)}, u32[]{:S(2)}) %copy-start.4) | copy-done | bytes 524312
  6.9 54.2 %shard_map.129 = (bf16[16,16384]{1,0:T(8,128)(2,1)S(1)}, bf16[16,16384]{1,0:T(8,128)(2,1)S(1)}, bf16[16,16384]{1,0:T(8,128)(2,1)S(1)}, f32[2,16384]{1,0:T(2,128)S(1)}) custom-call(bf16[16,16384]{1,0:T(8,128)(2,1)S(1)} %copy-done.2, bf16[16,16384]{1,0:T(8,128)(2,1)S(1)} %copy-done.3, bf16[16,16384]{1,0:T(8,128)(2,1)S(1)} %copy-done.4, ...), custom_call_target="tpu_custom_call" | custom-call | tf_op jit(solution)/shard_map/pallas_call | solution.py:311
  61.2 0.8 %copy.19 = bf16[16,16384]{1,0:T(8,128)(2,1)} copy(bf16[16,16384]{1,0:T(8,128)(2,1)S(1)} %get-tuple-element.8) | data formatting | bytes 1048576
  62.0 0.8 %copy.20 = bf16[16,16384]{1,0:T(8,128)(2,1)} copy(bf16[16,16384]{1,0:T(8,128)(2,1)S(1)} %get-tuple-element.9) | data formatting | bytes 1048576
  62.8 0.8 %copy.21 = bf16[16,16384]{1,0:T(8,128)(2,1)} copy(bf16[16,16384]{1,0:T(8,128)(2,1)S(1)} %get-tuple-element.10) | data formatting | bytes 1048576
  63.6 0.7 %copy.22 = f32[2,16384]{1,0:T(2,128)} copy(f32[2,16384]{1,0:T(2,128)S(1)} %get-tuple-element.11) | data formatting | bytes 262144
Async XLA Ops:
  1.4 1.2 %copy-start = (f32[16,16384]{1,0:T(8,128)S(1)}, f32[16,16384]{1,0:T(8,128)}, u32[]{:S(2)}) copy-start(f32[16,16384]{1,0:T(8,128)} %taps_hbm.1) | copy-start | bytes 3145732
  2.6 1.2 %copy-start.1 = (bf16[1024,512]{1,0:T(8,128)(2,1)S(1)}, bf16[1024,512]{1,0:T(8,128)(2,1)}, u32[]{:S(2)}) copy-start(bf16[1024,512]{1,0:T(8,128)(2,1)} %constant.15.first_hbm) | copy-start | bytes 3145732
  3.8 1.0 %copy-start.2 = (bf16[16,16384]{1,0:T(8,128)(2,1)S(1)}, bf16[16,16384]{1,0:T(8,128)(2,1)}, u32[]{:S(2)}) copy-start(bf16[16,16384]{1,0:T(8,128)(2,1)} %sig_hbm.1) | copy-start | bytes 1572868
  4.9 1.0 %copy-start.3 = (bf16[16,16384]{1,0:T(8,128)(2,1)S(1)}, bf16[16,16384]{1,0:T(8,128)(2,1)}, u32[]{:S(2)}) copy-start(bf16[16,16384]{1,0:T(8,128)(2,1)} %gate_hbm.1) | copy-start | bytes 1572868
  5.9 1.0 %copy-start.4 = (bf16[16,16384]{1,0:T(8,128)(2,1)S(1)}, bf16[16,16384]{1,0:T(8,128)(2,1)}, u32[]{:S(2)}) copy-start(bf16[16,16384]{1,0:T(8,128)(2,1)} %cot_hbm.1) | copy-start | bytes 1572868

commit v3 on v2

--- a/solution.py
+++ b/solution.py
@@ -39,21 +39,24 @@
 
 def kernel(
     shards, chs, rows, block,
-    sig_hbm, gate_hbm, cot_hbm, skip_ref, taps_hbm, first_hbm, second_hbm, back_hbm, twc_hbm, tws_hbm,
+    sig_hbm, gate_hbm, cot_hbm, gain_hbm, taps_hbm, first_hbm, second_hbm, back_hbm, twc_hbm, tws_hbm,
     out_ref, ggate_ref, gsig_ref, gtaps_ref,
-    sig, gate, cot, taps, first, second, back, twc, tws,
-    flat, send, recv, spec, both, stack, ysend, yrecv,
-    load_sem, send_sem, recv_sem,
+    sig, gate, cot, gain, taps, first, second, back, twc, tws,
+    flat, send, recv, hsend, hgrid, spec, both, stack, ysend, yrecv, tparts, tsend, trecv,
+    load_sem, send_sem, recv_sem, share_send, share_recv,
 ):
     me = lax.axis_index("ctx")
     ch = lax.axis_index("ch")
     own = shards // chs
+    tiles = N2 // 128
+    quarter = shards // tiles
+    hi, lo = ch // tiles, lax.rem(ch, tiles)
 
     loads = [
         pltpu.make_async_copy(src, dst, load_sem.at[i])
         for i, (src, dst) in enumerate(
-            [(sig_hbm, sig), (taps_hbm, taps), (gate_hbm, gate), (cot_hbm, cot), (first_hbm, first),
-             (twc_hbm, twc), (tws_hbm, tws), (second_hbm, second), (back_hbm, back)]
+            [(taps_hbm, taps), (sig_hbm, sig), (gate_hbm, gate), (cot_hbm, cot), (first_hbm, first),
+             (twc_hbm, twc), (tws_hbm, tws), (second_hbm, second), (back_hbm, back), (gain_hbm, gain)]
         )
     ]
     for load in loads:
@@ -70,8 +73,19 @@
     def is_self(peer_ctx, peer_ch):
         return jnp.logical_and(peer_ctx == me, peer_ch == ch)
 
-    def greet_owners(at, carry):
-        peer_ctx, peer_ch = own * ch + lax.rem(at, own), at // own
+    def greet_line(step, carry):
+        peer = hi * tiles + lax.rem(lo + step, tiles)
+        pl.semaphore_signal(barrier, inc=1, device_id={"ch": peer}, device_id_type=MESH)
+        return carry
+
+    lax.fori_loop(1, tiles, greet_line, 0)
+    alone = jnp.logical_and(me // own == ch, me // quarter == lo)
+
+    def source(at):
+        return own * ch + lax.rem(at, own), at // own * tiles + me // quarter
+
+    def greet_sources(at, carry):
+        peer_ctx, peer_ch = source(at)
 
         @pl.when(jnp.logical_not(is_self(peer_ctx, peer_ch)))
         def _():
@@ -81,7 +95,7 @@
 
         return carry
 
-    lax.fori_loop(0, shards, greet_owners, 0)
+    lax.fori_loop(0, quarter, greet_sources, 0)
 
     def spread(which, value_at):
         def one(row, carry):
@@ -90,7 +104,7 @@
                 flat[lane, pl.ds(row, shards, stride=rows), :] = value_at(cols)
             return carry
 
-        lax.fori_loop(0, rows, one, 0)
+        lax.fori_loop(0, rows, one, 0, unroll=8)
 
         def cast(at, carry):
             here = pl.ds(pl.multiple_of(at * rows, rows), rows)
@@ -98,7 +112,7 @@
                 send[which, at, :, lane * 128 : (lane + 1) * 128] = flat[lane, here, :].astype(jnp.bfloat16)
             return carry
 
-        lax.fori_loop(0, shards, cast, 0)
+        lax.fori_loop(0, shards, cast, 0, unroll=4)
 
     def remote(src, dst, which, slot_out, slot_in, device):
         return pltpu.make_async_remote_copy(
@@ -137,10 +151,10 @@
         here = pl.ds(pl.multiple_of(at * block, block), block)
         return here, twc[here, :], tws[here, :]
 
-    def forward(which):
+    def forward(which, load_grid):
         def one(at, carry):
             here, cos, sin = twist(at)
-            grid = recv[which].reshape(HALF, N2)
+            grid = load_grid()
             re = dot(first[here, :], grid)
             im = dot(first[pl.ds(pl.multiple_of(HALF + at * block, block), block), :], grid)
             both[:, :N2] = (re * cos + im * sin).astype(jnp.bfloat16)
@@ -180,68 +194,99 @@
 
         lax.fori_loop(0, HALF // block, last, 0)
 
+    def share(step):
+        return lax.rem(lo + step, tiles)
+
+    def taps_columns(step):
+        return pltpu.make_async_remote_copy(
+            src_ref=hgrid.at[lo], dst_ref=hgrid.at[lo], send_sem=share_send.at[0, step],
+            recv_sem=share_recv.at[0, step], device_id={"ch": hi * tiles + share(step)}, device_id_type=MESH,
+        )
+
+    def tap_terms(step):
+        return pltpu.make_async_remote_copy(
+            src_ref=ysend.at[2, pl.ds(share(step) * quarter, quarter)], dst_ref=tparts.at[step],
+            send_sem=share_send.at[1, step], recv_sem=share_recv.at[1, step],
+            device_id={"ch": hi * tiles + share(step)}, device_id_type=MESH,
+        )
+
     loads[0].wait()
+
+    def column(row, carry):
+        cols = pl.ds(pl.multiple_of(row * N2 + lo * 128, 128), 128)
+        flat[0, pl.ds(row, shards, stride=rows), :] = taps[:, cols]
+        return carry
+
+    lax.fori_loop(0, rows, column, 0, unroll=8)
+
+    def cast_column(at, carry):
+        hsend[at] = flat[0, pl.ds(pl.multiple_of(at * rows, rows), rows), :].astype(jnp.bfloat16)
+        return carry
+
+    lax.fori_loop(0, shards, cast_column, 0, unroll=4)
+    pl.semaphore_wait(barrier, shards - 1 + tiles - 1 + quarter - jnp.where(alone, 1, 0))
+    exchange(1, hsend, hgrid.at[lo])
+    loads[1].wait()
     spread(0, lambda cols: sig[:, cols].astype(jnp.float32))
-    pl.semaphore_wait(barrier, 2 * shards - 1 - jnp.where(me // own == ch, 1, 0))
     exchange(0, send.at[0], recv.at[0])
-    loads[1].wait()
-    spread(1, lambda cols: taps[:, cols])
-    exchange(1, send.at[1], recv.at[1])
     loads[2].wait()
     loads[3].wait()
-    spread(2, lambda cols: gate[:, cols].astype(jnp.float32) * cot[:, cols].astype(jnp.float32))
-    exchange(2, send.at[2], recv.at[2])
+    spread(1, lambda cols: gate[:, cols].astype(jnp.float32) * cot[:, cols].astype(jnp.float32))
+    exchange(2, send.at[1], recv.at[1])
     for load in loads[4:]:
         load.wait()
+    arrive(1, hsend, hgrid.at[lo])
+    for step in range(1, tiles):
+        taps_columns(step).start()
     arrive(0, send.at[0], recv.at[0])
-    forward(0)
-    arrive(1, send.at[1], recv.at[1])
-    forward(1)
+    forward(0, lambda: recv[0].reshape(HALF, N2))
+    for step in range(1, tiles):
+        taps_columns(step).wait_recv()
+    forward(1, lambda: jnp.concatenate([hgrid[tile].reshape(HALF, 128) for tile in range(tiles)], axis=1))
     inverse(0, 0, 1, False)
     exchange(3, ysend.at[0], yrecv.at[0])
-    arrive(2, send.at[2], recv.at[2])
-    forward(2)
+    arrive(2, send.at[1], recv.at[1])
+    forward(2, lambda: recv[1].reshape(HALF, N2))
+    inverse(2, 2, 0, True)
+    for step in range(1, tiles):
+        tap_terms(step).start()
     inverse(1, 2, 1, True)
     exchange(4, ysend.at[1], yrecv.at[1])
-    inverse(2, 2, 0, True)
-
-    mine = lax.rem(me, own) + own * ch
+
+    for step in range(1, tiles):
+        tap_terms(step).wait_recv()
+    for at in range(quarter):
+        total = ysend[2, lo * quarter + at].astype(jnp.float32)
+        for step in range(1, tiles):
+            total = total + tparts[step, at].astype(jnp.float32)
+        tsend[at] = total.astype(jnp.bfloat16)
+
+    slot = hi * own + lax.rem(me, own)
     owner = me // own
 
-    def give(step, wait):
-        peer = lax.rem(me + step, shards)
+    def give(at, wait):
+        peer = lo * quarter + at
         local = is_self(peer, owner)
 
         @pl.when(local)
         def _():
-            copy = pltpu.make_async_copy(ysend.at[2, peer], yrecv.at[2, mine], recv_sem.at[5, mine])
+            copy = pltpu.make_async_copy(tsend.at[at], trecv.at[slot], recv_sem.at[5, slot])
             copy.wait() if wait else copy.start()
 
         @pl.when(jnp.logical_not(local))
         def _():
-            copy = remote(ysend.at[2, peer], yrecv.at[2, mine], 5, peer, mine, {"ctx": peer, "ch": owner})
+            copy = remote(tsend.at[at], trecv.at[slot], 5, at, slot, {"ctx": peer, "ch": owner})
             copy.wait_send() if wait else copy.start()
 
-    def give_start(step, carry):
-        give(step, False)
-        return carry
-
-    def give_wait(step, carry):
-        give(step, True)
-        return carry
-
-    def take(at, carry):
-        peer_ctx, peer_ch = own * ch + lax.rem(at, own), at // own
+    for at in range(quarter):
+        give(at, False)
+
+    def take(at):
+        peer_ctx, peer_ch = source(at)
 
         @pl.when(jnp.logical_not(is_self(peer_ctx, peer_ch)))
         def _():
-            remote(
-                ysend.at[2, 0], yrecv.at[2, at], 5, 0, at, {"ctx": peer_ctx, "ch": peer_ch}
-            ).wait_recv()
-
-        return carry
-
-    lax.fori_loop(0, shards, give_start, 0)
+            remote(tsend.at[0], trecv.at[at], 5, 0, at, {"ctx": peer_ctx, "ch": peer_ch}).wait_recv()
 
     def gather(slot):
         def one(at, carry):
@@ -250,9 +295,12 @@
                 flat[lane, here, :] = yrecv[slot, at, :, lane * 128 : (lane + 1) * 128].astype(jnp.float32)
             return carry
 
-        lax.fori_loop(0, shards, one, 0)
-
-    skip = skip_ref[...]
+        lax.fori_loop(0, shards, one, 0, unroll=4)
+
+    channel = lax.broadcasted_iota(jnp.int32, (shards, 128), 0)
+    skip = jnp.zeros((shards, 128), jnp.float32)
+    for at in range(shards):
+        skip = jnp.where(channel == at, gain[at], skip)
     arrive(3, ysend.at[0], yrecv.at[0])
     gather(0)
 
@@ -264,7 +312,7 @@
             ggate_ref[:, cols] = (cot[:, cols].astype(jnp.float32) * mixed).astype(jnp.bfloat16)
         return carry
 
-    lax.fori_loop(0, rows, finish_conv, 0)
+    lax.fori_loop(0, rows, finish_conv, 0, unroll=8)
     arrive(4, ysend.at[1], yrecv.at[1])
     gather(1)
 
@@ -276,14 +324,16 @@
             gsig_ref[:, cols] = (corr + skip * upstream).astype(jnp.bfloat16)
         return carry
 
-    lax.fori_loop(0, rows, finish_corr, 0)
-    lax.fori_loop(0, shards, give_wait, 0)
-    lax.fori_loop(0, shards, take, 0)
+    lax.fori_loop(0, rows, finish_corr, 0, unroll=8)
+    for at in range(quarter):
+        give(at, True)
+    for at in range(quarter):
+        take(at)
     scale = 1.0 / math.sqrt(SEQ)
     for group in range(own):
-        total = yrecv[2, group].astype(jnp.float32)
-        for at in range(1, chs):
-            total = total + yrecv[2, own * at + group].astype(jnp.float32)
+        total = trecv[group].astype(jnp.float32)
+        for at in range(own + group, quarter, own):
+            total = total + trecv[at].astype(jnp.float32)
         for lane in range(N2 // 128):
             flat[lane, group * rows : (group + 1) * rows, :] = total[:, lane * 128 : (lane + 1) * 128] * scale
 
@@ -293,11 +343,23 @@
             gtaps_ref[:, cols] = flat[lane, pl.ds(row, own, stride=rows), :]
         return carry
 
-    lax.fori_loop(0, rows, finish_taps, 0)
-    for which in range(3):
-        drain(which, send.at[which], recv.at[which])
+    lax.fori_loop(0, rows, finish_taps, 0, unroll=8)
+    drain(1, hsend, hgrid.at[lo])
+    drain(0, send.at[0], recv.at[0])
+    drain(2, send.at[1], recv.at[1])
+    for step in range(1, tiles):
+        taps_columns(step).wait_send()
+        tap_terms(step).wait_send()
     drain(3, ysend.at[0], yrecv.at[0])
     drain(4, ysend.at[1], yrecv.at[1])
+
+
+def emit(*refs):
+    copies = [pltpu.make_async_copy(refs[at], refs[4 + at], refs[8].at[at]) for at in range(4)]
+    for copy in copies:
+        copy.start()
+    for copy in copies:
+        copy.wait()
 
 
 def body(shards, chs, signal, gate, cotangent, skip_gain, filter_taps):
@@ -308,16 +370,18 @@
     bf16, f32 = jnp.bfloat16, jnp.float32
     hbm = pl.BlockSpec(memory_space=pl.ANY)
     vmem = pl.BlockSpec(memory_space=pltpu.VMEM)
-    return pl.pallas_call(
+    operands = signal, gate, cotangent, skip_gain, filter_taps, *tables()
+    results = pl.pallas_call(
         functools.partial(kernel, shards, chs, rows, block),
         out_shape=[jax.ShapeDtypeStruct((channels, positions), bf16)] * 3
         + [jax.ShapeDtypeStruct((own, positions), f32)],
-        in_specs=[hbm] * 3 + [vmem] + [hbm] * 6,
+        in_specs=[hbm] * 10,
         out_specs=[vmem] * 4,
         scratch_shapes=[
             pltpu.VMEM((channels, positions), bf16),
             pltpu.VMEM((channels, positions), bf16),
             pltpu.VMEM((channels, positions), bf16),
+            pltpu.SMEM((channels,), f32),
             pltpu.VMEM((channels, positions), f32),
             pltpu.VMEM((2 * HALF, HALF), bf16),
             pltpu.VMEM((5 * N2, N2), bf16),
@@ -325,21 +389,36 @@
             pltpu.VMEM((HALF, N2), f32),
             pltpu.VMEM((HALF, N2), f32),
             pltpu.VMEM((N2 // 128, HALF, 128), f32),
-            pltpu.VMEM((3, shards, rows, N2), bf16),
-            pltpu.VMEM((3, shards, rows, N2), bf16),
+            pltpu.VMEM((2, shards, rows, N2), bf16),
+            pltpu.VMEM((2, shards, rows, N2), bf16),
+            pltpu.VMEM((shards, rows, 128), bf16),
+            pltpu.VMEM((N2 // 128, shards, rows, 128), bf16),
             pltpu.VMEM((3, 2, HALF, N2), f32),
             pltpu.VMEM((block, 2 * N2), bf16),
             pltpu.VMEM((2 * HALF, N2), bf16),
             pltpu.VMEM((3, shards, rows, N2), bf16),
-            pltpu.VMEM((3, shards, rows, N2), bf16),
-            pltpu.SemaphoreType.DMA((9,)),
+            pltpu.VMEM((2, shards, rows, N2), bf16),
+            pltpu.VMEM((N2 // 128, shards * 128 // N2, rows, N2), bf16),
+            pltpu.VMEM((shards * 128 // N2, rows, N2), bf16),
+            pltpu.VMEM((shards * 128 // N2, rows, N2), bf16),
+            pltpu.SemaphoreType.DMA((10,)),
             pltpu.SemaphoreType.DMA((6, shards)),
             pltpu.SemaphoreType.DMA((6, shards)),
+            pltpu.SemaphoreType.DMA((2, N2 // 128)),
+            pltpu.SemaphoreType.DMA((2, N2 // 128)),
         ],
         compiler_params=pltpu.CompilerParams(
             collective_id=0, has_side_effects=True, vmem_limit_bytes=48 * 1024 * 1024
         ),
-    )(signal, gate, cotangent, skip_gain.reshape(channels, 1), filter_taps, *tables())
+    )(*[pltpu.with_memory_space_constraint(operand, pltpu.HBM) for operand in operands])
+    return pl.pallas_call(
+        emit,
+        out_shape=[jax.ShapeDtypeStruct(result.shape, result.dtype) for result in results],
+        in_specs=[hbm] * 4,
+        out_specs=[hbm] * 4,
+        scratch_shapes=[pltpu.SemaphoreType.DMA((4,))],
+        compiler_params=pltpu.CompilerParams(vmem_limit_bytes=1024 * 1024),
+    )(*results)
 
 
 def solution(mesh):

time: 64.5 us -> 50.2 us (0.78)
  the two profiles are of different devices: /device:TPU:17 before, /device:TPU:25 now
where the time goes in v3:
time: 50.2 us; the launch traced here: 50.1 us
  Pallas kernels  49.4 us (98%)
  between operations  0.64 us (1%)
    pallas_call x1, Pallas kernels, body(): pl.pallas_call(functools.partial(kernel, shards, chs, rows, block), out_s...  48.2 us
    pallas_call x1, Pallas kernels, body(): pl.pallas_call(emit, out_shape=[jax.ShapeDtypeStruct(result.shape, result...  1.21 us

profile of v3, /device:TPU:25, one launch (start us, length us, event | category | flops | bytes accessed | tf_op | source)
XLA Modules:
  0.0 50.1 jit_solution(18244431426174972629)
XLA Ops:
  0.6 48.2 %shard_map.129 = (bf16[16,16384]{1,0:T(8,128)(2,1)S(1)}, bf16[16,16384]{1,0:T(8,128)(2,1)S(1)}, bf16[16,16384]{1,0:T(8,128)(2,1)S(1)}, f32[2,16384]{1,0:T(2,128)S(1)}) custom-call(bf16[16,16384]{1,0:T(8,128)(2,1)} %sig_hbm.1, bf16[16,16384]{1,0:T(8,128)(2,1)} %gate_hbm.1, bf16[16,16384]{1,0:T(8,128)(2,1)} %cot_hbm.1, f32[16]{0:T(128)} %gain_hbm.1, ...), custom_call_target="tpu_custom_call" | custom-call | tf_op jit(solution)/shard_map/pallas_call | solution.py:374
  48.9 1.2 %shard_map.130 = (bf16[16,16384]{1,0:T(8,128)(2,1)}, bf16[16,16384]{1,0:T(8,128)(2,1)}, bf16[16,16384]{1,0:T(8,128)(2,1)}, f32[2,16384]{1,0:T(2,128)}) custom-call(bf16[16,16384]{1,0:T(8,128)(2,1)S(1)} %get-tuple-element.8.refs_0_, bf16[16,16384]{1,0:T(8,128)(2,1)S(1)} %get-tuple-element.9.refs_1_, bf16[16,16384]{1,0:T(8,128)(2,1)S(1)} %get-tuple-element.10.refs_2_, ...), custom_call_target="tpu_custom_call" | custom-call | tf_op jit(solution)/shard_map/pallas_call | solution.py:414

commit v4 on v3

--- a/solution.py
+++ b/solution.py
@@ -18,19 +18,24 @@
 
 
 def tables():
+    quart, pair = HALF // 2, N2 // 2
+    k1 = np.arange(quart, dtype=np.int64)
     n1 = np.arange(HALF, dtype=np.int64)
-    k1 = np.arange(HALF, dtype=np.int64)
     n2 = np.arange(N2, dtype=np.int64)
+    rows = np.concatenate([k1, HALF - 1 - k1])
     ang_a = ((2 * k1 + 1)[:, None] * n1[None, :] % (2 * N1)) * (math.pi / N1)
-    ang_b = (n2[:, None] * n2[None, :] % N2) * (2.0 * math.pi / N2)
-    ang_t = ((2 * k1 + 1)[:, None] * n2[None, :] % (2 * POINTS)) * (math.pi / POINTS)
+    ang_b = (n2[:, None] * n2[None, : pair + 1] % N2) * (2.0 * math.pi / N2)
+    ang_t = ((2 * rows + 1)[:, None] * n2[None, :] % (2 * POINTS)) * (math.pi / POINTS)
     first = np.concatenate([np.cos(ang_a), -np.sin(ang_a)], axis=0)
+    first = np.stack([first[:, 0::2], first[:, 1::2]])
     cos_b, sin_b = np.cos(ang_b), np.sin(ang_b)
-    second = np.concatenate([cos_b, sin_b, cos_b, -sin_b, cos_b], axis=0)
-    back_first = 2.0 / POINTS * np.concatenate([np.cos(ang_a).T, -np.sin(ang_a).T], axis=1)
-    half = lambda a: jnp.asarray(a.astype(np.float32)).astype(jnp.bfloat16)
+    second = np.concatenate([cos_b[:, :pair], cos_b[:, pair:], sin_b[:, 1:pair]], axis=1)
+    half = lambda a: jnp.asarray(np.ascontiguousarray(a).astype(np.float32)).astype(jnp.bfloat16)
     full = lambda a: jnp.asarray(a.astype(np.float32))
-    return half(first), half(second), half(back_first), full(np.cos(ang_t)), full(np.sin(ang_t))
+    return (
+        half(first), half(second), half(second.T), half(2.0 / POINTS * first.transpose(0, 2, 1)),
+        full(np.cos(ang_t)), full(np.sin(ang_t)),
+    )
 
 
 def dot(a, b):
@@ -39,9 +44,9 @@
 
 def kernel(
     shards, chs, rows, block,
-    sig_hbm, gate_hbm, cot_hbm, gain_hbm, taps_hbm, first_hbm, second_hbm, back_hbm, twc_hbm, tws_hbm,
+    sig_hbm, gate_hbm, cot_hbm, gain_hbm, taps_hbm, first_hbm, second_hbm, under_hbm, back_hbm, twc_hbm, tws_hbm,
     out_ref, ggate_ref, gsig_ref, gtaps_ref,
-    sig, gate, cot, gain, taps, first, second, back, twc, tws,
+    sig, gate, cot, gain, taps, first, second, under, back, twc, tws,
     flat, send, recv, hsend, hgrid, spec, both, stack, ysend, yrecv, tparts, tsend, trecv,
     load_sem, send_sem, recv_sem, share_send, share_recv,
 ):
@@ -56,7 +61,7 @@
         pltpu.make_async_copy(src, dst, load_sem.at[i])
         for i, (src, dst) in enumerate(
             [(taps_hbm, taps), (sig_hbm, sig), (gate_hbm, gate), (cot_hbm, cot), (first_hbm, first),
-             (twc_hbm, twc), (tws_hbm, tws), (second_hbm, second), (back_hbm, back), (gain_hbm, gain)]
+             (twc_hbm, twc), (tws_hbm, tws), (second_hbm, second), (under_hbm, under), (back_hbm, back), (gain_hbm, gain)]
         )
     ]
     for load in loads:
@@ -97,11 +102,14 @@
 
     lax.fori_loop(0, quarter, greet_sources, 0)
 
+    def place(row):
+        return row // 2 + lax.rem(row, 2) * (rows // 2)
+
     def spread(which, value_at):
         def one(row, carry):
             for lane in range(N2 // 128):
                 cols = pl.ds(pl.multiple_of(row * N2 + lane * 128, 128), 128)
-                flat[lane, pl.ds(row, shards, stride=rows), :] = value_at(cols)
+                flat[lane, pl.ds(place(row), shards, stride=rows), :] = value_at(cols)
             return carry
 
         lax.fori_loop(0, rows, one, 0, unroll=8)
@@ -120,79 +128,95 @@
             device_id=device, device_id_type=MESH,
         )
 
+    def peer_of(step):
+        return lax.rem(me + step, shards)
+
+    def outgoing(which, src, dst, peer):
+        return remote(src.at[peer], dst.at[me], which, peer, me, {"ctx": peer})
+
+    def each(first, last, action):
+        def one(step, carry):
+            action(step)
+            return carry
+
+        lax.fori_loop(first, last, one, 0, unroll=True)
+
+    def keep(which, src, dst):
+        return pltpu.make_async_copy(src.at[me], dst.at[me], recv_sem.at[which, me])
+
     def exchange(which, src, dst):
-        def one(step, carry):
-            peer = lax.rem(me + step, shards)
-            remote(src.at[peer], dst.at[me], which, peer, me, {"ctx": peer}).start()
-            return carry
-
-        pltpu.make_async_copy(src.at[me], dst.at[me], recv_sem.at[which, me]).start()
-        lax.fori_loop(1, shards, one, 0)
+        each(1, shards, lambda step: outgoing(which, src, dst, peer_of(step)).start())
+        keep(which, src, dst).start()
 
     def arrive(which, src, dst):
-        pltpu.make_async_copy(src.at[me], dst.at[me], recv_sem.at[which, me]).wait()
-
-        def one(step, carry):
-            peer = lax.rem(me + shards - step, shards)
+        keep(which, src, dst).wait()
+
+        def take_one(step):
+            peer = peer_of(step)
             remote(src.at[peer], dst.at[peer], which, peer, peer, {"ctx": peer}).wait_recv()
-            return carry
-
-        lax.fori_loop(1, shards, one, 0)
+
+        each(1, shards, take_one)
 
     def drain(which, src, dst):
-        def one(step, carry):
-            peer = lax.rem(me + step, shards)
-            remote(src.at[peer], dst.at[me], which, peer, me, {"ctx": peer}).wait_send()
-            return carry
-
-        lax.fori_loop(1, shards, one, 0)
-
-    def twist(at):
-        here = pl.ds(pl.multiple_of(at * block, block), block)
-        return here, twc[here, :], tws[here, :]
+        each(1, shards, lambda step: outgoing(which, src, dst, peer_of(step)).wait_send())
+
+    quart, pair = HALF // 2, N2 // 2
+    edge = lax.broadcasted_iota(jnp.int32, (block, pair), 1) == 0
 
     def forward(which, load_grid):
-        def one(at, carry):
-            here, cos, sin = twist(at)
-            grid = load_grid()
-            re = dot(first[here, :], grid)
-            im = dot(first[pl.ds(pl.multiple_of(HALF + at * block, block), block), :], grid)
-            both[:, :N2] = (re * cos + im * sin).astype(jnp.bfloat16)
-            both[:, N2:] = (im * cos - re * sin).astype(jnp.bfloat16)
-            spec[which, 0, here, :] = dot(both[...], second[: 2 * N2, :])
-            spec[which, 1, here, :] = dot(both[...], second[3 * N2 :, :])
-            return carry
-
-        lax.fori_loop(0, HALF // block, one, 0)
+        for at in range(quart // block):
+            here = slice(at * block, (at + 1) * block)
+            there = slice(quart + at * block, quart + (at + 1) * block)
+            even, odd = load_grid()
+            e_re, o_re = dot(first[0, here, :], even), dot(first[1, here, :], odd)
+            e_im, o_im = dot(first[0, there, :], even), dot(first[1, there, :], odd)
+            for part, rows_at, re, im in (
+                (0, here, e_re + o_re, e_im + o_im), (1, there, e_re - o_re, o_im - e_im)
+            ):
+                cos, sin = twc[rows_at, :], tws[rows_at, :]
+                both[at, part] = (re * cos + im * sin).astype(jnp.bfloat16)
+                both[at, 2 + part] = (im * cos - re * sin).astype(jnp.bfloat16)
+            summed = dot(both[at].reshape(4 * block, N2), second[...]).reshape(4, block, N2)
+            for part, rows_at in ((0, here), (1, there)):
+                r_c, r_s = summed[part][:, :pair], summed[part][:, pair:]
+                i_c, i_s = summed[2 + part][:, :pair], summed[2 + part][:, pair:]
+                spec[which, 0, rows_at, :pair] = jnp.where(edge, r_c, r_c + i_s)
+                spec[which, 0, rows_at, pair:] = jnp.where(edge, r_s, r_c - i_s)
+                spec[which, 1, rows_at, :pair] = jnp.where(edge, i_c, i_c - r_s)
+                spec[which, 1, rows_at, pair:] = jnp.where(edge, i_s, i_c + r_s)
+
+    def product(left, right, conj, rows_at, cols):
+        l_re, l_im = spec[left, 0, rows_at, cols], spec[left, 1, rows_at, cols]
+        r_re, r_im = spec[right, 0, rows_at, cols], spec[right, 1, rows_at, cols]
+        if conj:
+            return l_re * r_re + l_im * r_im, l_im * r_re - l_re * r_im
+        return l_re * r_re - l_im * r_im, l_re * r_im + l_im * r_re
 
     def inverse(slot, left, right, conj):
-        def one(at, carry):
-            here, cos, sin = twist(at)
-            l_re, l_im = spec[left, 0, here, :], spec[left, 1, here, :]
-            r_re, r_im = spec[right, 0, here, :], spec[right, 1, here, :]
-            if conj:
-                re, im = l_re * r_re + l_im * r_im, l_im * r_re - l_re * r_im
-            else:
-                re, im = l_re * r_re - l_im * r_im, l_re * r_im + l_im * r_re
-            both[:, :N2] = re.astype(jnp.bfloat16)
-            both[:, N2:] = im.astype(jnp.bfloat16)
-            re = dot(both[...], second[2 * N2 : 4 * N2, :])
-            im = dot(both[...], second[N2 : 3 * N2, :])
-            stack[here, :] = (re * cos - im * sin).astype(jnp.bfloat16)
-            stack[pl.ds(pl.multiple_of(HALF + at * block, block), block), :] = (re * sin + im * cos).astype(
-                jnp.bfloat16
-            )
-            return carry
-
-        lax.fori_loop(0, HALF // block, one, 0)
-
-        def last(at, carry):
-            here = pl.ds(pl.multiple_of(at * block, block), block)
-            value = dot(back[here, :], stack[...]).astype(jnp.bfloat16)
-            ysend[slot, pl.ds(at * (block // rows), block // rows)] = value.reshape(block // rows, rows, N2)
-            return carry
-
-        lax.fori_loop(0, HALF // block, last, 0)
+        for at in range(quart // block):
+            here = slice(at * block, (at + 1) * block)
+            there = slice(quart + at * block, quart + (at + 1) * block)
+            for part, rows_at in ((0, here), (1, there)):
+                lo_re, lo_im = product(left, right, conj, rows_at, slice(0, pair))
+                hi_re, hi_im = product(left, right, conj, rows_at, slice(pair, N2))
+                both[at, part, :, :pair] = jnp.where(edge, lo_re, lo_re + hi_re).astype(jnp.bfloat16)
+                both[at, part, :, pair:] = jnp.where(edge, hi_re, hi_im - lo_im).astype(jnp.bfloat16)
+                both[at, 2 + part, :, :pair] = jnp.where(edge, lo_im, lo_im + hi_im).astype(jnp.bfloat16)
+                both[at, 2 + part, :, pair:] = jnp.where(edge, hi_im, lo_re - hi_re).astype(jnp.bfloat16)
+            summed = dot(both[at].reshape(4 * block, N2), under[...]).reshape(4, block, N2)
+            twisted = []
+            for part, rows_at in ((0, here), (1, there)):
+                cos, sin = twc[rows_at, :], tws[rows_at, :]
+                re, im = summed[part], summed[2 + part]
+                twisted.append((re * cos - im * sin, re * sin + im * cos))
+            (lo_re, lo_im), (hi_re, hi_im) = twisted
+            stack[0, here, :] = (lo_re + hi_re).astype(jnp.bfloat16)
+            stack[0, there, :] = (lo_im - hi_im).astype(jnp.bfloat16)
+            stack[1, here, :] = (lo_re - hi_re).astype(jnp.bfloat16)
+            stack[1, there, :] = (lo_im + hi_im).astype(jnp.bfloat16)
+        for odd in range(2):
+            value = dot(back[odd], stack[odd]).astype(jnp.bfloat16)
+            ysend[slot, :, odd * (rows // 2) : (odd + 1) * (rows // 2)] = value.reshape(shards, rows // 2, N2)
 
     def share(step):
         return lax.rem(lo + step, tiles)
@@ -214,7 +238,7 @@
 
     def column(row, carry):
         cols = pl.ds(pl.multiple_of(row * N2 + lo * 128, 128), 128)
-        flat[0, pl.ds(row, shards, stride=rows), :] = taps[:, cols]
+        flat[0, pl.ds(place(row), shards, stride=rows), :] = taps[:, cols]
         return carry
 
     lax.fori_loop(0, rows, column, 0, unroll=8)
@@ -224,29 +248,40 @@
         return carry
 
     lax.fori_loop(0, shards, cast_column, 0, unroll=4)
+    loads[1].wait()
+    spread(0, lambda cols: sig[:, cols].astype(jnp.float32))
+    loads[2].wait()
+    loads[3].wait()
+    for load in loads[4:]:
+        load.wait()
     pl.semaphore_wait(barrier, shards - 1 + tiles - 1 + quarter - jnp.where(alone, 1, 0))
     exchange(1, hsend, hgrid.at[lo])
-    loads[1].wait()
-    spread(0, lambda cols: sig[:, cols].astype(jnp.float32))
     exchange(0, send.at[0], recv.at[0])
-    loads[2].wait()
-    loads[3].wait()
-    spread(1, lambda cols: gate[:, cols].astype(jnp.float32) * cot[:, cols].astype(jnp.float32))
-    exchange(2, send.at[1], recv.at[1])
-    for load in loads[4:]:
-        load.wait()
     arrive(1, hsend, hgrid.at[lo])
     for step in range(1, tiles):
         taps_columns(step).start()
+
+    spread(1, lambda cols: gate[:, cols].astype(jnp.float32) * cot[:, cols].astype(jnp.float32))
+    exchange(2, send.at[1], recv.at[1])
     arrive(0, send.at[0], recv.at[0])
-    forward(0, lambda: recv[0].reshape(HALF, N2))
+
+    def arrived(which):
+        return [
+            recv[which, :, odd * (rows // 2) : (odd + 1) * (rows // 2), :].reshape(HALF // 2, N2) for odd in range(2)
+        ]
+
+    def arrived_taps():
+        tile = lambda at, odd: hgrid[at, :, odd * (rows // 2) : (odd + 1) * (rows // 2), :].reshape(HALF // 2, 128)
+        return [jnp.concatenate([tile(at, odd) for at in range(tiles)], axis=1) for odd in range(2)]
+
+    forward(0, lambda: arrived(0))
     for step in range(1, tiles):
         taps_columns(step).wait_recv()
-    forward(1, lambda: jnp.concatenate([hgrid[tile].reshape(HALF, 128) for tile in range(tiles)], axis=1))
+    forward(1, arrived_taps)
     inverse(0, 0, 1, False)
     exchange(3, ysend.at[0], yrecv.at[0])
     arrive(2, send.at[1], recv.at[1])
-    forward(2, lambda: recv[1].reshape(HALF, N2))
+    forward(2, lambda: arrived(1))
     inverse(2, 2, 0, True)
     for step in range(1, tiles):
         tap_terms(step).start()
@@ -307,7 +342,7 @@
     def finish_conv(row, carry):
         for lane in range(N2 // 128):
             cols = pl.ds(pl.multiple_of(row * N2 + lane * 128, 128), 128)
-            mixed = flat[lane, pl.ds(row, shards, stride=rows), :] + skip * sig[:, cols].astype(jnp.float32)
+            mixed = flat[lane, pl.ds(place(row), shards, stride=rows), :] + skip * sig[:, cols].astype(jnp.float32)
             out_ref[:, cols] = (gate[:, cols].astype(jnp.float32) * mixed).astype(jnp.bfloat16)
             ggate_ref[:, cols] = (cot[:, cols].astype(jnp.float32) * mixed).astype(jnp.bfloat16)
         return carry
@@ -320,7 +355,7 @@
         for lane in range(N2 // 128):
             cols = pl.ds(pl.multiple_of(row * N2 + lane * 128, 128), 128)
             upstream = gate[:, cols].astype(jnp.float32) * cot[:, cols].astype(jnp.float32)
-            corr = flat[lane, pl.ds(row, shards, stride=rows), :]
+            corr = flat[lane, pl.ds(place(row), shards, stride=rows), :]
             gsig_ref[:, cols] = (corr + skip * upstream).astype(jnp.bfloat16)
         return carry
 
@@ -340,7 +375,7 @@
     def finish_taps(row, carry):
         for lane in range(N2 // 128):
             cols = pl.ds(pl.multiple_of(row * N2 + lane * 128, 128), 128)
-            gtaps_ref[:, cols] = flat[lane, pl.ds(row, own, stride=rows), :]
+            gtaps_ref[:, cols] = flat[lane, pl.ds(place(row), own, stride=rows), :]
         return carry
 
     lax.fori_loop(0, rows, finish_taps, 0, unroll=8)
@@ -366,7 +401,7 @@
     channels, positions = signal.shape
     rows = positions // N2
     own = shards // chs
-    block = 256
+    block = 128
     bf16, f32 = jnp.bfloat16, jnp.float32
     hbm = pl.BlockSpec(memory_space=pl.ANY)
     vmem = pl.BlockSpec(memory_space=pltpu.VMEM)
@@ -375,7 +410,7 @@
         functools.partial(kernel, shards, chs, rows, block),
         out_shape=[jax.ShapeDtypeStruct((channels, positions), bf16)] * 3
         + [jax.ShapeDtypeStruct((own, positions), f32)],
-        in_specs=[hbm] * 10,
+        in_specs=[hbm] * 11,
         out_specs=[vmem] * 4,
         scratch_shapes=[
             pltpu.VMEM((channels, positions), bf16),
@@ -383,9 +418,10 @@
             pltpu.VMEM((channels, positions), bf16),
             pltpu.SMEM((channels,), f32),
             pltpu.VMEM((channels, positions), f32),
-            pltpu.VMEM((2 * HALF, HALF), bf16),
-            pltpu.VMEM((5 * N2, N2), bf16),
-            pltpu.VMEM((HALF, 2 * HALF), bf16),
+            pltpu.VMEM((2, HALF, HALF // 2), bf16),
+            pltpu.VMEM((N2, N2), bf16),
+            pltpu.VMEM((N2, N2), bf16),
+            pltpu.VMEM((2, HALF // 2, HALF), bf16),
             pltpu.VMEM((HALF, N2), f32),
             pltpu.VMEM((HALF, N2), f32),
             pltpu.VMEM((N2 // 128, HALF, 128), f32),
@@ -394,14 +430,14 @@
             pltpu.VMEM((shards, rows, 128), bf16),
             pltpu.VMEM((N2 // 128, shards, rows, 128), bf16),
             pltpu.VMEM((3, 2, HALF, N2), f32),
-            pltpu.VMEM((block, 2 * N2), bf16),
-            pltpu.VMEM((2 * HALF, N2), bf16),
+            pltpu.VMEM((HALF // 2 // block, 4, block, N2), bf16),
+            pltpu.VMEM((2, HALF, N2), bf16),
             pltpu.VMEM((3, shards, rows, N2), bf16),
             pltpu.VMEM((2, shards, rows, N2), bf16),
             pltpu.VMEM((N2 // 128, shards * 128 // N2, rows, N2), bf16),
             pltpu.VMEM((shards * 128 // N2, rows, N2), bf16),
             pltpu.VMEM((shards * 128 // N2, rows, N2), bf16),
-            pltpu.SemaphoreType.DMA((10,)),
+            pltpu.SemaphoreType.DMA((11,)),
             pltpu.SemaphoreType.DMA((6, shards)),
             pltpu.SemaphoreType.DMA((6, shards)),
             pltpu.SemaphoreType.DMA((2, N2 // 128)),

time: 50.2 us -> 46.1 us (0.918)
  Pallas kernels: 49.4 us -> 44.8 us
    pallas_call x1, Pallas kernels: 48.2 us -> 43.6 us  [body(): pl.pallas_call(functools.partial(kernel, shards, chs, rows, block), out_s...]
where the time goes in v4:
time: 46.1 us; the launch traced here: 45.5 us
  Pallas kernels  44.8 us (97%)
  between operations  0.64 us (1%)
    pallas_call x1, Pallas kernels, body(): pl.pallas_call(functools.partial(kernel, shards, chs, rows, block), out_s...  43.6 us
    pallas_call x1, Pallas kernels, body(): pl.pallas_call(emit, out_shape=[jax.ShapeDtypeStruct(result.shape, result...  1.21 us

profile of v4, /device:TPU:25, one launch (start us, length us, event | category | flops | bytes accessed | tf_op | source)
XLA Modules:
  0.0 45.5 jit_solution(4694379915793819050)
XLA Ops:
  0.6 43.6 %shard_map.138 = (bf16[16,16384]{1,0:T(8,128)(2,1)S(1)}, bf16[16,16384]{1,0:T(8,128)(2,1)S(1)}, bf16[16,16384]{1,0:T(8,128)(2,1)S(1)}, f32[2,16384]{1,0:T(2,128)S(1)}) custom-call(bf16[16,16384]{1,0:T(8,128)(2,1)} %sig_hbm.1, bf16[16,16384]{1,0:T(8,128)(2,1)} %gate_hbm.1, bf16[16,16384]{1,0:T(8,128)(2,1)} %cot_hbm.1, f32[16]{0:T(128)} %gain_hbm.1, ...), custom_call_target="tpu_custom_call" | custom-call | tf_op jit(solution)/shard_map/pallas_call | solution.py:409
  44.3 1.2 %shard_map.139 = (bf16[16,16384]{1,0:T(8,128)(2,1)}, bf16[16,16384]{1,0:T(8,128)(2,1)}, bf16[16,16384]{1,0:T(8,128)(2,1)}, f32[2,16384]{1,0:T(2,128)}) custom-call(bf16[16,16384]{1,0:T(8,128)(2,1)S(1)} %get-tuple-element.8.refs_0_, bf16[16,16384]{1,0:T(8,128)(2,1)S(1)} %get-tuple-element.9.refs_1_, bf16[16,16384]{1,0:T(8,128)(2,1)S(1)} %get-tuple-element.10.refs_2_, ...), custom_call_target="tpu_custom_call" | custom-call | tf_op jit(solution)/shard_map/pallas_call | solution.py:450

commit v5 on v4

--- a/solution.py
+++ b/solution.py
@@ -48,7 +48,7 @@
     out_ref, ggate_ref, gsig_ref, gtaps_ref,
     sig, gate, cot, gain, taps, first, second, under, back, twc, tws,
     flat, send, recv, hsend, hgrid, spec, both, stack, ysend, yrecv, tparts, tsend, trecv,
-    load_sem, send_sem, recv_sem, share_send, share_recv,
+    load_sem, send_sem, recv_sem, share_send, share_recv, total_send, total_recv, ready,
 ):
     me = lax.axis_index("ctx")
     ch = lax.axis_index("ch")
@@ -78,29 +78,34 @@
     def is_self(peer_ctx, peer_ch):
         return jnp.logical_and(peer_ctx == me, peer_ch == ch)
 
-    def greet_line(step, carry):
-        peer = hi * tiles + lax.rem(lo + step, tiles)
-        pl.semaphore_signal(barrier, inc=1, device_id={"ch": peer}, device_id_type=MESH)
-        return carry
-
-    lax.fori_loop(1, tiles, greet_line, 0)
-    alone = jnp.logical_and(me // own == ch, me // quarter == lo)
+    owner = me // own
 
     def source(at):
-        return own * ch + lax.rem(at, own), at // own * tiles + me // quarter
-
-    def greet_sources(at, carry):
+        return own * ch + at % own, at // own * tiles + me // quarter
+
+    def signal(sem, condition, device):
+        @pl.when(condition)
+        def _():
+            pl.semaphore_signal(sem, inc=1, device_id=device, device_id_type=MESH)
+
+    for step in range(1, tiles):
+        peer = lax.rem(lo + step, tiles)
+        signal(barrier, peer > lo, {"ch": hi * tiles + peer})
+    for at in range(quarter):
         peer_ctx, peer_ch = source(at)
-
-        @pl.when(jnp.logical_not(is_self(peer_ctx, peer_ch)))
-        def _():
-            pl.semaphore_signal(
-                barrier, inc=1, device_id={"ctx": peer_ctx, "ch": peer_ch}, device_id_type=MESH
-            )
-
-        return carry
-
-    lax.fori_loop(0, quarter, greet_sources, 0)
+        signal(barrier, peer_ch > ch, {"ctx": peer_ctx, "ch": peer_ch})
+        signal(barrier, owner > ch, {"ctx": lo * quarter + at, "ch": owner})
+    awaited = shards - 1 + lo + jnp.where(owner < ch, quarter, 0)
+    for at in range(0, quarter, own):
+        awaited = awaited + jnp.where(source(at)[1] < ch, own, 0)
+
+    def answer():
+        for step in range(1, tiles):
+            peer = lax.rem(lo + step, tiles)
+            signal(ready.at[0], peer < lo, {"ch": hi * tiles + peer})
+        for at in range(quarter):
+            peer_ctx, peer_ch = source(at)
+            signal(ready.at[1], peer_ch < ch, {"ctx": peer_ctx, "ch": peer_ch})
 
     def place(row):
         return row // 2 + lax.rem(row, 2) * (rows // 2)
@@ -122,17 +127,14 @@
 
         lax.fori_loop(0, shards, cast, 0, unroll=4)
 
-    def remote(src, dst, which, slot_out, slot_in, device):
+    def remote(src, dst, which, device):
         return pltpu.make_async_remote_copy(
-            src_ref=src, dst_ref=dst, send_sem=send_sem.at[which, slot_out], recv_sem=recv_sem.at[which, slot_in],
+            src_ref=src, dst_ref=dst, send_sem=send_sem.at[which], recv_sem=recv_sem.at[which],
             device_id=device, device_id_type=MESH,
         )
 
     def peer_of(step):
         return lax.rem(me + step, shards)
-
-    def outgoing(which, src, dst, peer):
-        return remote(src.at[peer], dst.at[me], which, peer, me, {"ctx": peer})
 
     def each(first, last, action):
         def one(step, carry):
@@ -141,24 +143,20 @@
 
         lax.fori_loop(first, last, one, 0, unroll=True)
 
-    def keep(which, src, dst):
-        return pltpu.make_async_copy(src.at[me], dst.at[me], recv_sem.at[which, me])
-
     def exchange(which, src, dst):
-        each(1, shards, lambda step: outgoing(which, src, dst, peer_of(step)).start())
-        keep(which, src, dst).start()
-
-    def arrive(which, src, dst):
-        keep(which, src, dst).wait()
-
-        def take_one(step):
+        def one(step):
             peer = peer_of(step)
-            remote(src.at[peer], dst.at[peer], which, peer, peer, {"ctx": peer}).wait_recv()
-
-        each(1, shards, take_one)
-
-    def drain(which, src, dst):
-        each(1, shards, lambda step: outgoing(which, src, dst, peer_of(step)).wait_send())
+            remote(src.at[peer], dst.at[me], which, {"ctx": peer}).start()
+
+        each(1, shards, one)
+        pltpu.make_async_copy(src.at[me], dst.at[me], recv_sem.at[which]).start()
+
+    def arrive(which, dst):
+        pltpu.make_async_copy(dst, dst, recv_sem.at[which]).wait()
+
+    def drain(which, src):
+        sent = src.at[1:shards]
+        pltpu.make_async_copy(sent, sent, send_sem.at[which]).wait()
 
     quart, pair = HALF // 2, N2 // 2
     edge = lax.broadcasted_iota(jnp.int32, (block, pair), 1) == 0
@@ -221,11 +219,16 @@
     def share(step):
         return lax.rem(lo + step, tiles)
 
-    def taps_columns(step):
+    def taps_columns(at):
+        peer = hi * tiles + lax.rem(lo + (1, tiles - 1)[at], tiles)
         return pltpu.make_async_remote_copy(
-            src_ref=hgrid.at[lo], dst_ref=hgrid.at[lo], send_sem=share_send.at[0, step],
-            recv_sem=share_recv.at[0, step], device_id={"ch": hi * tiles + share(step)}, device_id_type=MESH,
+            src_ref=hgrid.at[at], dst_ref=hgrid.at[3 - at], send_sem=share_send.at[0, at],
+            recv_sem=share_recv.at[0, at], device_id={"ch": peer}, device_id_type=MESH,
         )
+
+    def taps_out(step):
+        peer = peer_of(step)
+        remote(hsend.at[:, peer], hgrid.at[0:2, me], 1, {"ctx": peer}).start()
 
     def tap_terms(step):
         return pltpu.make_async_remote_copy(
@@ -237,50 +240,58 @@
     loads[0].wait()
 
     def column(row, carry):
-        cols = pl.ds(pl.multiple_of(row * N2 + lo * 128, 128), 128)
-        flat[0, pl.ds(place(row), shards, stride=rows), :] = taps[:, cols]
+        for at in range(2):
+            cols = pl.ds(pl.multiple_of(row * N2 + lax.rem(lo + at, tiles) * 128, 128), 128)
+            flat[at, pl.ds(place(row), shards, stride=rows), :] = taps[:, cols]
         return carry
 
     lax.fori_loop(0, rows, column, 0, unroll=8)
 
     def cast_column(at, carry):
-        hsend[at] = flat[0, pl.ds(pl.multiple_of(at * rows, rows), rows), :].astype(jnp.bfloat16)
+        for part in range(2):
+            hsend[part, at] = flat[part, pl.ds(pl.multiple_of(at * rows, rows), rows), :].astype(jnp.bfloat16)
         return carry
 
     lax.fori_loop(0, shards, cast_column, 0, unroll=4)
+    pl.semaphore_wait(barrier, awaited)
+    each(1, shards, taps_out)
+    pltpu.make_async_copy(hsend.at[:, me], hgrid.at[0:2, me], recv_sem.at[1]).start()
     loads[1].wait()
     spread(0, lambda cols: sig[:, cols].astype(jnp.float32))
+    exchange(0, send.at[0], recv.at[0])
+    answer()
+    arrive(1, hgrid.at[0:2])
+
+    @pl.when(lo < tiles - 1)
+    def _():
+        pl.semaphore_wait(ready.at[0], tiles - 1 - lo)
+
+    for at in range(2):
+        taps_columns(at).start()
+
     loads[2].wait()
     loads[3].wait()
+    spread(1, lambda cols: gate[:, cols].astype(jnp.float32) * cot[:, cols].astype(jnp.float32))
+    exchange(2, send.at[1], recv.at[1])
     for load in loads[4:]:
         load.wait()
-    pl.semaphore_wait(barrier, shards - 1 + tiles - 1 + quarter - jnp.where(alone, 1, 0))
-    exchange(1, hsend, hgrid.at[lo])
-    exchange(0, send.at[0], recv.at[0])
-    arrive(1, hsend, hgrid.at[lo])
-    for step in range(1, tiles):
-        taps_columns(step).start()
-
-    spread(1, lambda cols: gate[:, cols].astype(jnp.float32) * cot[:, cols].astype(jnp.float32))
-    exchange(2, send.at[1], recv.at[1])
-    arrive(0, send.at[0], recv.at[0])
-
     def arrived(which):
         return [
             recv[which, :, odd * (rows // 2) : (odd + 1) * (rows // 2), :].reshape(HALF // 2, N2) for odd in range(2)
         ]
 
     def arrived_taps():
-        tile = lambda at, odd: hgrid[at, :, odd * (rows // 2) : (odd + 1) * (rows // 2), :].reshape(HALF // 2, 128)
+        tile = lambda at, odd: hgrid[lax.rem(at + tiles - lo, tiles), :, odd * (rows // 2) : (odd + 1) * (rows // 2), :].reshape(HALF // 2, 128)
         return [jnp.concatenate([tile(at, odd) for at in range(tiles)], axis=1) for odd in range(2)]
 
+    for at in range(2):
+        taps_columns(at).wait_recv()
+    forward(1, arrived_taps)
+    arrive(0, recv.at[0])
     forward(0, lambda: arrived(0))
-    for step in range(1, tiles):
-        taps_columns(step).wait_recv()
-    forward(1, arrived_taps)
     inverse(0, 0, 1, False)
     exchange(3, ysend.at[0], yrecv.at[0])
-    arrive(2, send.at[1], recv.at[1])
+    arrive(2, recv.at[1])
     forward(2, lambda: arrived(1))
     inverse(2, 2, 0, True)
     for step in range(1, tiles):
@@ -288,6 +299,37 @@
     inverse(1, 2, 1, True)
     exchange(4, ysend.at[1], yrecv.at[1])
 
+    sent = hsend.at[:, 1:shards]
+    pltpu.make_async_copy(sent, sent, send_sem.at[1]).wait()
+    drain(0, send.at[0])
+    drain(2, send.at[1])
+    for at in range(2):
+        taps_columns(at).wait_send()
+    def gather(slot):
+        def one(at, carry):
+            here = pl.ds(pl.multiple_of(at * rows, rows), rows)
+            for lane in range(N2 // 128):
+                flat[lane, here, :] = yrecv[slot, at, :, lane * 128 : (lane + 1) * 128].astype(jnp.float32)
+            return carry
+
+        lax.fori_loop(0, shards, one, 0, unroll=4)
+
+    channel = lax.broadcasted_iota(jnp.int32, (shards, 128), 0)
+    skip = jnp.zeros((shards, 128), jnp.float32)
+    for at in range(shards):
+        skip = jnp.where(channel == at, gain[at], skip)
+    arrive(3, yrecv.at[0])
+    gather(0)
+
+    def finish_conv(row, carry):
+        for lane in range(N2 // 128):
+            cols = pl.ds(pl.multiple_of(row * N2 + lane * 128, 128), 128)
+            mixed = flat[lane, pl.ds(place(row), shards, stride=rows), :] + skip * sig[:, cols].astype(jnp.float32)
+            out_ref[:, cols] = (gate[:, cols].astype(jnp.float32) * mixed).astype(jnp.bfloat16)
+            ggate_ref[:, cols] = (cot[:, cols].astype(jnp.float32) * mixed).astype(jnp.bfloat16)
+        return carry
+
+    lax.fori_loop(0, rows, finish_conv, 0, unroll=8)
     for step in range(1, tiles):
         tap_terms(step).wait_recv()
     for at in range(quarter):
@@ -296,8 +338,15 @@
             total = total + tparts[step, at].astype(jnp.float32)
         tsend[at] = total.astype(jnp.bfloat16)
 
+    for step in range(1, tiles):
+        tap_terms(step).wait_send()
     slot = hi * own + lax.rem(me, own)
-    owner = me // own
+
+    def tap_total(at, device):
+        return pltpu.make_async_remote_copy(
+            src_ref=tsend.at[at], dst_ref=trecv.at[slot], send_sem=total_send.at[at], recv_sem=total_recv.at[slot],
+            device_id=device, device_id_type=MESH,
+        )
 
     def give(at, wait):
         peer = lo * quarter + at
@@ -305,50 +354,30 @@
 
         @pl.when(local)
         def _():
-            copy = pltpu.make_async_copy(tsend.at[at], trecv.at[slot], recv_sem.at[5, slot])
+            copy = pltpu.make_async_copy(tsend.at[at], trecv.at[slot], total_recv.at[slot])
             copy.wait() if wait else copy.start()
 
         @pl.when(jnp.logical_not(local))
         def _():
-            copy = remote(tsend.at[at], trecv.at[slot], 5, at, slot, {"ctx": peer, "ch": owner})
+            copy = tap_total(at, {"ctx": peer, "ch": owner})
             copy.wait_send() if wait else copy.start()
+
+    def take(at):
+        peer_ctx, peer_ch = source(at)
+
+        @pl.when(jnp.logical_not(is_self(peer_ctx, peer_ch)))
+        def _():
+            pltpu.make_async_copy(tsend.at[0], trecv.at[at], total_recv.at[at]).wait()
+
+
+    @pl.when(owner > ch)
+    def _():
+        pl.semaphore_wait(ready.at[1], quarter)
 
     for at in range(quarter):
         give(at, False)
-
-    def take(at):
-        peer_ctx, peer_ch = source(at)
-
-        @pl.when(jnp.logical_not(is_self(peer_ctx, peer_ch)))
-        def _():
-            remote(tsend.at[0], trecv.at[at], 5, 0, at, {"ctx": peer_ctx, "ch": peer_ch}).wait_recv()
-
-    def gather(slot):
-        def one(at, carry):
-            here = pl.ds(pl.multiple_of(at * rows, rows), rows)
-            for lane in range(N2 // 128):
-                flat[lane, here, :] = yrecv[slot, at, :, lane * 128 : (lane + 1) * 128].astype(jnp.float32)
-            return carry
-
-        lax.fori_loop(0, shards, one, 0, unroll=4)
-
-    channel = lax.broadcasted_iota(jnp.int32, (shards, 128), 0)
-    skip = jnp.zeros((shards, 128), jnp.float32)
-    for at in range(shards):
-        skip = jnp.where(channel == at, gain[at], skip)
-    arrive(3, ysend.at[0], yrecv.at[0])
-    gather(0)
-
-    def finish_conv(row, carry):
-        for lane in range(N2 // 128):
-            cols = pl.ds(pl.multiple_of(row * N2 + lane * 128, 128), 128)
-            mixed = flat[lane, pl.ds(place(row), shards, stride=rows), :] + skip * sig[:, cols].astype(jnp.float32)
-            out_ref[:, cols] = (gate[:, cols].astype(jnp.float32) * mixed).astype(jnp.bfloat16)
-            ggate_ref[:, cols] = (cot[:, cols].astype(jnp.float32) * mixed).astype(jnp.bfloat16)
-        return carry
-
-    lax.fori_loop(0, rows, finish_conv, 0, unroll=8)
-    arrive(4, ysend.at[1], yrecv.at[1])
+    drain(3, ysend.at[0])
+    arrive(4, yrecv.at[1])
     gather(1)
 
     def finish_corr(row, carry):
@@ -379,14 +408,7 @@
         return carry
 
     lax.fori_loop(0, rows, finish_taps, 0, unroll=8)
-    drain(1, hsend, hgrid.at[lo])
-    drain(0, send.at[0], recv.at[0])
-    drain(2, send.at[1], recv.at[1])
-    for step in range(1, tiles):
-        taps_columns(step).wait_send()
-        tap_terms(step).wait_send()
-    drain(3, ysend.at[0], yrecv.at[0])
-    drain(4, ysend.at[1], yrecv.at[1])
+    drain(4, ysend.at[1])
 
 
 def emit(*refs):
@@ -427,7 +449,7 @@
             pltpu.VMEM((N2 // 128, HALF, 128), f32),
             pltpu.VMEM((2, shards, rows, N2), bf16),
             pltpu.VMEM((2, shards, rows, N2), bf16),
-            pltpu.VMEM((shards, rows, 128), bf16),
+            pltpu.VMEM((2, shards, rows, 128), bf16),
             pltpu.VMEM((N2 // 128, shards, rows, 128), bf16),
             pltpu.VMEM((3, 2, HALF, N2), f32),
             pltpu.VMEM((HALF // 2 // block, 4, block, N2), bf16),
@@ -438,10 +460,13 @@
             pltpu.VMEM((shards * 128 // N2, rows, N2), bf16),
             pltpu.VMEM((shards * 128 // N2, rows, N2), bf16),
             pltpu.SemaphoreType.DMA((11,)),
-            pltpu.SemaphoreType.DMA((6, shards)),
-            pltpu.SemaphoreType.DMA((6, shards)),
+            pltpu.SemaphoreType.DMA((5,)),
+            pltpu.SemaphoreType.DMA((5,)),
             pltpu.SemaphoreType.DMA((2, N2 // 128)),
             pltpu.SemaphoreType.DMA((2, N2 // 128)),
+            pltpu.SemaphoreType.DMA((shards * 128 // N2,)),
+            pltpu.SemaphoreType.DMA((shards * 128 // N2,)),
+            pltpu.SemaphoreType.REGULAR((2,)),
         ],
         compiler_params=pltpu.CompilerParams(
             collective_id=0, has_side_effects=True, vmem_limit_bytes=48 * 1024 * 1024

time: 46.1 us -> 44.4 us (0.963); the launches traced: 45.5 us -> 44.3 us
  Pallas kernels: 44.8 us -> 43.7 us
    pallas_call x1, Pallas kernels: 43.6 us -> 42.5 us  [body(): pl.pallas_call(functools.partial(kernel, shards, chs, rows, block), out_s...]
where the time goes in v5:
time: 44.4 us; the launch traced here: 44.3 us
  Pallas kernels  43.7 us (98%)
  between operations  0.64 us (1%)
    pallas_call x1, Pallas kernels, body(): pl.pallas_call(functools.partial(kernel, shards, chs, rows, block), out_s...  42.5 us
    pallas_call x1, Pallas kernels, body(): pl.pallas_call(emit, out_shape=[jax.ShapeDtypeStruct(result.shape, result...  1.21 us

profile of v5, /device:TPU:25, one launch (start us, length us, event | category | flops | bytes accessed | tf_op | source)
XLA Modules:
  0.0 44.3 jit_solution(17386907384548216348)
XLA Ops:
  0.6 42.5 %shard_map.138 = (bf16[16,16384]{1,0:T(8,128)(2,1)S(1)}, bf16[16,16384]{1,0:T(8,128)(2,1)S(1)}, bf16[16,16384]{1,0:T(8,128)(2,1)S(1)}, f32[2,16384]{1,0:T(2,128)S(1)}) custom-call(bf16[16,16384]{1,0:T(8,128)(2,1)} %sig_hbm.1, bf16[16,16384]{1,0:T(8,128)(2,1)} %gate_hbm.1, bf16[16,16384]{1,0:T(8,128)(2,1)} %cot_hbm.1, f32[16]{0:T(128)} %gain_hbm.1, ...), custom_call_target="tpu_custom_call" | custom-call | tf_op jit(solution)/shard_map/pallas_call | solution.py:431
  43.1 1.2 %shard_map.139 = (bf16[16,16384]{1,0:T(8,128)(2,1)}, bf16[16,16384]{1,0:T(8,128)(2,1)}, bf16[16,16384]{1,0:T(8,128)(2,1)}, f32[2,16384]{1,0:T(2,128)}) custom-call(bf16[16,16384]{1,0:T(8,128)(2,1)S(1)} %get-tuple-element.8.refs_0_, bf16[16,16384]{1,0:T(8,128)(2,1)S(1)} %get-tuple-element.9.refs_1_, bf16[16,16384]{1,0:T(8,128)(2,1)S(1)} %get-tuple-element.10.refs_2_, ...), custom_call_target="tpu_custom_call" | custom-call | tf_op jit(solution)/shard_map/pallas_call | solution.py:475

commit v6 on v5

--- a/solution.py
+++ b/solution.py
@@ -237,6 +237,13 @@
             device_id={"ch": hi * tiles + share(step)}, device_id_type=MESH,
         )
 
+    def tap_term(step, at):
+        return pltpu.make_async_remote_copy(
+            src_ref=ysend.at[2, share(step) * quarter + at], dst_ref=tparts.at[step, at],
+            send_sem=share_send.at[1, step], recv_sem=share_recv.at[1, step],
+            device_id={"ch": hi * tiles + share(step)}, device_id_type=MESH,
+        )
+
     loads[0].wait()
 
     def column(row, carry):
@@ -294,8 +301,9 @@
     arrive(2, recv.at[1])
     forward(2, lambda: arrived(1))
     inverse(2, 2, 0, True)
-    for step in range(1, tiles):
-        tap_terms(step).start()
+    for at in range(quarter):
+        for step in (2, 1, 3):
+            tap_term(step, at).start()
     inverse(1, 2, 1, True)
     exchange(4, ysend.at[1], yrecv.at[1])
 
@@ -318,6 +326,51 @@
     skip = jnp.zeros((shards, 128), jnp.float32)
     for at in range(shards):
         skip = jnp.where(channel == at, gain[at], skip)
+    for step in range(1, tiles):
+        tap_terms(step).wait_recv()
+    slot = hi * own + lax.rem(me, own)
+
+    def tap_total(at, device):
+        return pltpu.make_async_remote_copy(
+            src_ref=tsend.at[at], dst_ref=trecv.at[slot], send_sem=total_send.at[at], recv_sem=total_recv.at[slot],
+            device_id=device, device_id_type=MESH,
+        )
+
+    def give(at, wait):
+        peer = lo * quarter + at
+        local = is_self(peer, owner)
+
+        @pl.when(local)
+        def _():
+            copy = pltpu.make_async_copy(tsend.at[at], trecv.at[slot], total_recv.at[slot])
+            copy.wait() if wait else copy.start()
+
+        @pl.when(jnp.logical_not(local))
+        def _():
+            copy = tap_total(at, {"ctx": peer, "ch": owner})
+            copy.wait_send() if wait else copy.start()
+
+    def take(at):
+        peer_ctx, peer_ch = source(at)
+
+        @pl.when(jnp.logical_not(is_self(peer_ctx, peer_ch)))
+        def _():
+            pltpu.make_async_copy(tsend.at[0], trecv.at[at], total_recv.at[at]).wait()
+
+
+    @pl.when(owner > ch)
+    def _():
+        pl.semaphore_wait(ready.at[1], quarter)
+
+    for at in range(quarter):
+        total = ysend[2, lo * quarter + at].astype(jnp.float32)
+        for step in range(1, tiles):
+            total = total + tparts[step, at].astype(jnp.float32)
+        tsend[at] = total.astype(jnp.bfloat16)
+
+        give(at, False)
+    for step in range(1, tiles):
+        tap_terms(step).wait_send()
     arrive(3, yrecv.at[0])
     gather(0)
 
@@ -330,52 +383,6 @@
         return carry
 
     lax.fori_loop(0, rows, finish_conv, 0, unroll=8)
-    for step in range(1, tiles):
-        tap_terms(step).wait_recv()
-    for at in range(quarter):
-        total = ysend[2, lo * quarter + at].astype(jnp.float32)
-        for step in range(1, tiles):
-            total = total + tparts[step, at].astype(jnp.float32)
-        tsend[at] = total.astype(jnp.bfloat16)
-
-    for step in range(1, tiles):
-        tap_terms(step).wait_send()
-    slot = hi * own + lax.rem(me, own)
-
-    def tap_total(at, device):
-        return pltpu.make_async_remote_copy(
-            src_ref=tsend.at[at], dst_ref=trecv.at[slot], send_sem=total_send.at[at], recv_sem=total_recv.at[slot],
-            device_id=device, device_id_type=MESH,
-        )
-
-    def give(at, wait):
-        peer = lo * quarter + at
-        local = is_self(peer, owner)
-
-        @pl.when(local)
-        def _():
-            copy = pltpu.make_async_copy(tsend.at[at], trecv.at[slot], total_recv.at[slot])
-            copy.wait() if wait else copy.start()
-
-        @pl.when(jnp.logical_not(local))
-        def _():
-            copy = tap_total(at, {"ctx": peer, "ch": owner})
-            copy.wait_send() if wait else copy.start()
-
-    def take(at):
-        peer_ctx, peer_ch = source(at)
-
-        @pl.when(jnp.logical_not(is_self(peer_ctx, peer_ch)))
-        def _():
-            pltpu.make_async_copy(tsend.at[0], trecv.at[at], total_recv.at[at]).wait()
-
-
-    @pl.when(owner > ch)
-    def _():
-        pl.semaphore_wait(ready.at[1], quarter)
-
-    for at in range(quarter):
-        give(at, False)
     drain(3, ysend.at[0])
     arrive(4, yrecv.at[1])
     gather(1)

time: 44.4 us -> 44 us (level)
  Pallas kernels: 43.7 us -> 43.2 us
    pallas_call x1, Pallas kernels: 42.5 us -> 42 us  [body(): pl.pallas_call(functools.partial(kernel, shards, chs, rows, block), out_s...]
where the time goes in v6:
time: 44 us; the launch traced here: 43.8 us
  Pallas kernels  43.2 us (98%)
  between operations  0.64 us (1%)
    pallas_call x1, Pallas kernels, body(): pl.pallas_call(functools.partial(kernel, shards, chs, rows, block), out_s...  42 us
    pallas_call x1, Pallas kernels, body(): pl.pallas_call(emit, out_shape=[jax.ShapeDtypeStruct(result.shape, result...  1.21 us

profile of v6, /device:TPU:25, one launch (start us, length us, event | category | flops | bytes accessed | tf_op | source)
XLA Modules:
  0.0 43.8 jit_solution(7947007624903374837)
XLA Ops:
  0.6 42.0 %shard_map.138 = (bf16[16,16384]{1,0:T(8,128)(2,1)S(1)}, bf16[16,16384]{1,0:T(8,128)(2,1)S(1)}, bf16[16,16384]{1,0:T(8,128)(2,1)S(1)}, f32[2,16384]{1,0:T(2,128)S(1)}) custom-call(bf16[16,16384]{1,0:T(8,128)(2,1)} %sig_hbm.1, bf16[16,16384]{1,0:T(8,128)(2,1)} %gate_hbm.1, bf16[16,16384]{1,0:T(8,128)(2,1)} %cot_hbm.1, f32[16]{0:T(128)} %gain_hbm.1, ...), custom_call_target="tpu_custom_call" | custom-call | tf_op jit(solution)/shard_map/pallas_call | solution.py:438
  42.6 1.2 %shard_map.139 = (bf16[16,16384]{1,0:T(8,128)(2,1)}, bf16[16,16384]{1,0:T(8,128)(2,1)}, bf16[16,16384]{1,0:T(8,128)(2,1)}, f32[2,16384]{1,0:T(2,128)}) custom-call(bf16[16,16384]{1,0:T(8,128)(2,1)S(1)} %get-tuple-element.8.refs_0_, bf16[16,16384]{1,0:T(8,128)(2,1)S(1)} %get-tuple-element.9.refs_1_, bf16[16,16384]{1,0:T(8,128)(2,1)S(1)} %get-tuple-element.10.refs_2_, ...), custom_call_target="tpu_custom_call" | custom-call | tf_op jit(solution)/shard_map/pallas_call | solution.py:482

commit v7 on v6

--- a/solution.py
+++ b/solution.py
@@ -14,6 +14,7 @@
 SEQ = 262144
 HALF = N1 // 2
 POINTS = N1 * N2
+BLOCK = 256
 MESH = pl.DeviceIdType.MESH
 
 
@@ -28,12 +29,14 @@
     ang_t = ((2 * rows + 1)[:, None] * n2[None, :] % (2 * POINTS)) * (math.pi / POINTS)
     first = np.concatenate([np.cos(ang_a), -np.sin(ang_a)], axis=0)
     first = np.stack([first[:, 0::2], first[:, 1::2]])
+    back_first = 2.0 / POINTS * first.transpose(0, 2, 1)
+    first = first.reshape(2, 2, quart // BLOCK, BLOCK, quart).transpose(0, 2, 1, 3, 4).reshape(2, HALF, quart)
     cos_b, sin_b = np.cos(ang_b), np.sin(ang_b)
     second = np.concatenate([cos_b[:, :pair], cos_b[:, pair:], sin_b[:, 1:pair]], axis=1)
     half = lambda a: jnp.asarray(np.ascontiguousarray(a).astype(np.float32)).astype(jnp.bfloat16)
     full = lambda a: jnp.asarray(a.astype(np.float32))
     return (
-        half(first), half(second), half(second.T), half(2.0 / POINTS * first.transpose(0, 2, 1)),
+        half(first), half(second), half(second.T), half(back_first),
         full(np.cos(ang_t)), full(np.sin(ang_t)),
     )
 
@@ -166,8 +169,9 @@
             here = slice(at * block, (at + 1) * block)
             there = slice(quart + at * block, quart + (at + 1) * block)
             even, odd = load_grid()
-            e_re, o_re = dot(first[0, here, :], even), dot(first[1, here, :], odd)
-            e_im, o_im = dot(first[0, there, :], even), dot(first[1, there, :], odd)
+            twin = slice(2 * at * block, 2 * (at + 1) * block)
+            of_even, of_odd = dot(first[0, twin, :], even), dot(first[1, twin, :], odd)
+            e_re, e_im, o_re, o_im = of_even[:block], of_even[block:], of_odd[:block], of_odd[block:]
             for part, rows_at, re, im in (
                 (0, here, e_re + o_re, e_im + o_im), (1, there, e_re - o_re, o_im - e_im)
             ):
@@ -430,7 +434,7 @@
     channels, positions = signal.shape
     rows = positions // N2
     own = shards // chs
-    block = 128
+    block = BLOCK
     bf16, f32 = jnp.bfloat16, jnp.float32
     hbm = pl.BlockSpec(memory_space=pl.ANY)
     vmem = pl.BlockSpec(memory_space=pltpu.VMEM)

time: 44 us -> 44 us (level)
  no operation moved by 1% of the time
where the time goes in v7:
time: 44 us; the launch traced here: 43.9 us
  Pallas kernels  43.3 us (98%)
  between operations  0.64 us (1%)
    pallas_call x1, Pallas kernels, body(): pl.pallas_call(functools.partial(kernel, shards, chs, rows, block), out_s...  42.1 us
    pallas_call x1, Pallas kernels, body(): pl.pallas_call(emit, out_shape=[jax.ShapeDtypeStruct(result.shape, result...  1.21 us

profile of v7, /device:TPU:25, one launch (start us, length us, event | category | flops | bytes accessed | tf_op | source)
XLA Modules:
  0.0 43.9 jit_solution(6927831462690857943)
XLA Ops:
  0.6 42.1 %shard_map.138 = (bf16[16,16384]{1,0:T(8,128)(2,1)S(1)}, bf16[16,16384]{1,0:T(8,128)(2,1)S(1)}, bf16[16,16384]{1,0:T(8,128)(2,1)S(1)}, f32[2,16384]{1,0:T(2,128)S(1)}) custom-call(bf16[16,16384]{1,0:T(8,128)(2,1)} %sig_hbm.1, bf16[16,16384]{1,0:T(8,128)(2,1)} %gate_hbm.1, bf16[16,16384]{1,0:T(8,128)(2,1)} %cot_hbm.1, f32[16]{0:T(128)} %gain_hbm.1, ...), custom_call_target="tpu_custom_call" | custom-call | tf_op jit(solution)/shard_map/pallas_call | solution.py:442
  42.7 1.2 %shard_map.139 = (bf16[16,16384]{1,0:T(8,128)(2,1)}, bf16[16,16384]{1,0:T(8,128)(2,1)}, bf16[16,16384]{1,0:T(8,128)(2,1)}, f32[2,16384]{1,0:T(2,128)}) custom-call(bf16[16,16384]{1,0:T(8,128)(2,1)S(1)} %get-tuple-element.8.refs_0_, bf16[16,16384]{1,0:T(8,128)(2,1)S(1)} %get-tuple-element.9.refs_1_, bf16[16,16384]{1,0:T(8,128)(2,1)S(1)} %get-tuple-element.10.refs_2_, ...), custom_call_target="tpu_custom_call" | custom-call | tf_op jit(solution)/shard_map/pallas_call | solution.py:486
